TPU v7x, 128 devices: a whole 4x4x4 slice. The times are simulated.
128 devices in a mesh: lon: 8 (over x, z_hi), lat: 16 (over y, z_lo, core).
Axes of the slice: x: 4, y: 4, z: 4 (z_hi: 2, z_lo: 2; z = z_hi * 2 + z_lo), core: 2. Of those that a mesh axis runs over, the one named last changes fastest.
Arguments:
- tokens: bfloat16 [4, 192, 192, 192], P(None, 'lat', 'lon'), may hold values from -6 to 6
- gain_one: float32 [192], replicated, may hold values from 0.5 to 1.5
- w_qkv: bfloat16 [192, 576], replicated, may hold values from -0.4375 to 0.4375
- w_proj: bfloat16 [192, 192], replicated, may hold values from -0.4375 to 0.4375
- bias_table: float32 [16, 2, 6, 144, 144], P('lat'), may hold values from -4 to 4
- gain_two: float32 [192], replicated, may hold values from 0.5 to 1.5
- w_fc1: bfloat16 [192, 768], replicated, may hold values from -0.4375 to 0.4375
- w_fc2: bfloat16 [768, 192], replicated, may hold values from -0.21875 to 0.21875
- gain_merge: float32 [768], replicated, may hold values from 0.5 to 1.5
- w_merge: bfloat16 [768, 384], replicated, may hold values from -0.21875 to 0.21875
- cotangent: bfloat16 [4, 96, 96, 384], P(None, 'lat', 'lon'), may hold values from -6 to 6
Outputs:
- merged: bfloat16 [4, 96, 96, 384], P(None, 'lat', 'lon')
- grad_tokens: bfloat16 [4, 192, 192, 192], P(None, 'lat', 'lon')
- grad_qkv: float32 [192, 576], replicated
- grad_proj: float32 [192, 192], replicated
- grad_fc1: float32 [192, 768], replicated
- grad_fc2: float32 [768, 192], replicated
- grad_merge: float32 [768, 384], replicated
- grad_bias: float32 [16, 2, 6, 144, 144], P('lat')
All inputs are finite; a program needn't handle non-finite values.
Results may differ from a plain program's by a relative error of at most 0.02.
Values may be sent and summed in bfloat16 or wider, within the bound.
No kernel may reach another device: no remote copies, remote signals or barrier semaphores. Data moves between devices by JAX's collectives and lax.ppermute only.
A program may use at most 128 MiB of HBM per device.

v0:
```python
import functools

import jax
import jax.numpy as jnp
import numpy as np
from jax import lax
from jax.experimental import pallas as pl
from jax.experimental.pallas import tpu as pltpu
from jax.sharding import PartitionSpec as P

F32 = jnp.float32
BF16 = jnp.bfloat16
EPS = 1e-05
D = 192
HEADS = 6
HD = 32
WT = 144
HQ = HEADS * WT
FF = 768
MG = 384
SCALE = HD ** (-0.5)
OFF = -1e30
SCALAR = pl.BlockSpec(memory_space=pltpu.SMEM)
WHOLE = pl.BlockSpec(memory_space=pltpu.VMEM)
LAT = ("chip", "core")
GROUP = 8
PEERS = 64
FIRST = 40
SECOND = 48
ROWS = FIRST + SECOND
HALF = PEERS * FIRST
BIAS_AT = 960


def one_hot(shape, pairs):
    table = np.zeros(shape, np.float32)
    for row, col in pairs:
        table[row, col] = 1.0
    return jnp.asarray(table, BF16)


def pack_map():
    pairs = [(r * 9 + c, r * 24 + c) for r in range(6) for c in range(9)]
    pairs += [(56 + r * 3 + c, r * 24 + 21 + c) for r in range(6) for c in range(3)]
    return one_hot((80, 144), pairs)


def pack_cot_map():
    pairs = []
    for lev in range(4):
        for r in range(3):
            for c in range(12):
                pairs.append((lev * 96 + r * 16 + c, ((3 + r) * 12 + c) * 4 + lev))
                pairs.append((lev * 96 + 48 + r * 16 + c, (r * 12 + c) * 4 + lev))
            for c in range(2):
                pairs.append((384 + lev * 6 + r * 2 + c, ((3 + r) * 12 + c) * 4 + lev))
                pairs.append((408 + lev * 6 + r * 2 + c, (r * 12 + c) * 4 + lev))
    return one_hot((432, 288), pairs)


def window_map():
    pairs = []
    for win in range(6):
        for row in range(12):
            for c in range(6):
                e, r = 6 * win + c, row % 6
                upper = row < 6
                if e < 3:
                    src = (344 if upper else 424) + r * 3 + e
                elif e < 27:
                    src = (0 if upper else 144) + r * 24 + e - 3
                else:
                    src = (288 if upper else 368) + r * 9 + e - 27
                pairs.append((win * 72 + row * 6 + c, src))
    return one_hot((432, 448), pairs)


def cot_map():
    pairs = []
    for lev in range(4):
        for r in range(6):
            for p in range(13):
                if p < 11:
                    src = lev * 96 + r * 16 + p + 1
                else:
                    src = (384 if r < 3 else 408) + lev * 6 + r % 3 * 2 + p - 11
                pairs.append((lev * 80 + r * 13 + p, src))
    return one_hot((320, 432), pairs)


def quad_pairs():
    pairs = []
    for ro in range(2):
        for co in range(2):
            for pr in range(6):
                for p in range(13):
                    row, e = 2 * pr + ro, 5 + 2 * p + co
                    if e == 5:
                        src = 288 + row
                    elif e == 30:
                        src = 304 + row
                    else:
                        src = (e - 6) // 6 * 72 + row * 6 + (e - 6) % 6
                    pairs.append(((2 * ro + co) * 80 + pr * 13 + p, src))
    return pairs


def quad_map():
    return one_hot((320, 320), quad_pairs())


def back_map():
    return one_hot((288, 320), [(s, d) for d, s in quad_pairs() if s < 288])


def out_map():
    pairs = []
    for row in range(12):
        for e in range(24):
            src = e // 6 * 72 + row * 6 + e % 6
            r = row % 6
            if e < 21:
                dst = (0 if row < 6 else 144) + r * 24 + e + 3
            else:
                dst = (288 if row < 6 else 320) + r * 3 + e - 21
            pairs.append((dst, src))
    return one_hot((352, 288), pairs)


def merged_map():
    pairs = []
    for r in range(6):
        for p in range(11):
            pairs.append(((0 if r < 3 else 48) + r % 3 * 16 + p + 1, r * 13 + p))
        pairs.append(((96 if r < 3 else 112) + r % 3, r * 13 + 11))
    return one_hot((128, 80), pairs)


def place_map():
    return one_hot((144, 32), [(r * 24 + c, r * 3 + c) for r in range(6) for c in range(3)])


def place_merged_map():
    pairs = []
    for lev in range(4):
        for r in range(6):
            for c in range(12):
                if c:
                    src = (192 if r < 3 else 0) + lev * 48 + r % 3 * 16 + c
                else:
                    src = (448 if r < 3 else 384) + lev * 16 + r % 3
                pairs.append(((r * 12 + c) * 4 + lev, src))
    return one_hot((288, 512), pairs)


def head_mask():
    return one_hot((HQ, D), [(h * WT + q, h * HD + c) for h in range(HEADS) for q in range(WT) for c in range(HD)])


def fold_map():
    return one_hot((WT, HQ), [(q, h * WT + q) for h in range(HEADS) for q in range(WT)])


def side_mask():
    return one_hot((WT, D), [(h * 24 + q, h * HD + c) for h in range(HEADS) for q in range(24) for c in range(HD)])


def side_fold():
    pairs = [(li * 16 + r, h * 24 + li * 12 + r) for h in range(HEADS) for li in range(2) for r in range(12)]
    return one_hot((32, WT), pairs)


def side_pick(col, padded):
    step, heads = (16, 1) if padded else (12, HEADS)
    pairs = [
        (h * 2 * step + li * step + r, li * 72 + r * 6 + col)
        for h in range(heads)
        for li in range(2)
        for r in range(12)
    ]
    return one_hot((2 * step * heads, WT), pairs)


def nn(a, b):
    return lax.dot_general(a, b, (((1,), (0,)), ((), ())), preferred_element_type=F32)


def nt(a, b):
    return lax.dot_general(a, b, (((1,), (1,)), ((), ())), preferred_element_type=F32)


def tn(a, b):
    return lax.dot_general(a, b, (((0,), (0,)), ((), ())), preferred_element_type=F32)


def norm_parts(values):
    center = values - jnp.mean(values, axis=-1, keepdims=True)
    rstd = lax.rsqrt(jnp.mean(center * center, axis=-1, keepdims=True) + EPS)
    return center * rstd, rstd


def norm_back(hat, rstd, gain, upstream):
    g = upstream * gain
    return rstd * (g - jnp.mean(g, axis=-1, keepdims=True) - hat * jnp.mean(g * hat, axis=-1, keepdims=True))


LEVEL_AT = ((1, 1), (0, 0), (0, 1), (1, 0))


def pack_kernel(tok, cot, pmap, cmap, dn, rt, lf, dr, dl, here, rows, wide, narrow):
    for i in range(72):
        rows[4 * i : 4 * i + 4] = cot[i].astype(F32)
    c = nn(cmap[...], rows[...].astype(BF16))
    wide[...] = jnp.zeros_like(wide)
    narrow[...] = jnp.zeros_like(narrow)
    for lev in range(4):
        top = tok[lev, 0:144]
        dn[lev, 0:144] = top
        for side, block in enumerate((tok[lev, 144:288], top)):
            got = nn(pmap[...], block)
            wide[side, lev * 54 : lev * 54 + 54] = got[0:54]
            narrow[side, lev * 18 : lev * 18 + 18] = got[56:74]
        here[lev] = c[lev * 96 : lev * 96 + 48].astype(BF16)
        part = c[lev * 96 + 48 : lev * 96 + 96].astype(BF16)
        dn[lev, 144:192] = part[:, 0:D]
        dn[lev, 192:240] = part[:, D : 2 * D]
    for side in range(2):
        part = c[384 + 24 * side : 408 + 24 * side]
        wide[side, 216:240] = part[:, 0:D]
        wide[side, 240:264] = part[:, D : 2 * D]
    rt[...] = wide[0].astype(BF16)
    dr[...] = wide[1].astype(BF16)
    lf[...] = narrow[0].astype(BF16)
    dl[...] = narrow[1].astype(BF16)


def label(pos, z, bottom):
    row = ((pos % 72 >= 36) & bottom).astype(jnp.int32)
    return row + (2 * (pos // 72).astype(jnp.int32) if z == 1 else 0)


def split_weights(wqkv, w3, wt3):
    eye = (lax.broadcasted_iota(jnp.int32, (D, D), 0) == lax.broadcasted_iota(jnp.int32, (D, D), 1)).astype(BF16)
    for part in range(3):
        w = wqkv[:, part * D : (part + 1) * D]
        w3[part] = w
        wt3[part] = nt(eye, w).astype(BF16)


def first_kernel(
    core_ref, bottom_ref, own, dn, rt, lf, dr, dl, cot, bias, gain_one, wqkv, wproj, gain_two, wfc1, wfc2t, gain_merge, wmerge,
    m_win, m_cot, m_quad, m_back, m_head, m_headt, m_fold, m_side, m_sidet, m_sfold, m_pick, m_there,
    stay, leave, merged, tok8, xn, prob, dout,
    grads, w3, wt3, bias_t, low_cols, high_cols, halo, mixed, tok, side, resq, mlpin, act, dgel, blk, dresq, resw, cotq,
):
    split_weights(wqkv, w3, wt3)
    bottom = bottom_ref[0, 0] > 0
    lane = lax.broadcasted_iota(jnp.int32, (1, HQ), 1) % WT
    row = lax.broadcasted_iota(jnp.int32, (WT, 1), 0)
    for z in range(2):
        bias_t[z] = jnp.where(label(row, z, bottom) != label(lane, z, bottom), OFF, bias[z].T)
        low_cols[z] = bias[z, :, 0:128]
        high_cols[z, :, 0 : WT - 128] = bias[z, :, 128:WT]

    halo[...] = jnp.zeros_like(halo)
    rt_, lf_, dr_, dl_ = (ref[...].astype(F32) for ref in (rt, lf, dr, dl))
    for lev in range(4):
        z, li = LEVEL_AT[lev]
        halo[0:54] = rt_[lev * 54 : lev * 54 + 54]
        halo[56:74] = lf_[lev * 18 : lev * 18 + 18]
        halo[80:134] = dr_[lev * 54 : lev * 54 + 54]
        halo[136:154] = dl_[lev * 18 : lev * 18 + 18]
        src = jnp.concatenate([own[lev, 144:288], dn[lev, 0:144], halo[...].astype(BF16)], axis=0)
        got = nn(m_win[...], src)
        for win in range(6):
            tok[z * 6 + win, li * 72 : li * 72 + 72] = got[win * 72 : win * 72 + 72]

    g1 = gain_one[...]

    def forward(i, carry):
        ws = [i * GROUP + n for n in range(GROUP)]
        zs = [w // 4 for w in ws]
        ts = [tok[z * 6 + w % 4 + 1] for w, z in zip(ws, zs)]
        xs = [(norm_parts(t)[0] * g1).astype(BF16) for t in ts]
        for w, t, x in zip(ws, ts, xs):
            tok8[w] = t.astype(BF16)
            xn[w] = x
        qs = [nn(x, w3[0]).astype(BF16) for x in xs]
        ks = [nn(x, w3[1]).astype(BF16) for x in xs]
        vts = [nt(wt3[2], x).astype(BF16) for x in xs]
        ss = [nt(k, jnp.concatenate([q] * HEADS, axis=0) * m_head[...]) for q, k in zip(qs, ks)]
        ps = []
        for w, z, score in zip(ws, zs, ss):
            e = jnp.exp(score * SCALE + bias_t[z])
            p = (e * (1.0 / jnp.sum(e, axis=0, keepdims=True))).astype(BF16)
            prob[w] = p
            ps.append(p)
        fulls = [nn(vt, p).astype(BF16) * m_headt[...] for vt, p in zip(vts, ps)]
        mxs = [nt(m_fold[...], full).astype(BF16) for full in fulls]
        for w, t, mx in zip(ws, ts, mxs):
            mixed[w] = mx
            att = nn(mx, wproj[...]).astype(BF16)
            resw[w] = (t + att.astype(F32)).astype(BF16).astype(F32)
        return carry

    lax.fori_loop(0, 8 // GROUP, forward, 0)

    lane = lax.broadcasted_iota(jnp.int32, (1, WT), 1) % 24
    lane = lane // 12 * 72 + lane % 12 * 6
    beside = [(n, z) for n in range(2) for z in range(2)]
    ts = [tok[z * 6 + 5 * n] for n, z in beside]
    xs = [(norm_parts(t)[0] * g1).astype(BF16) for t in ts]
    qs = [nn(x, w3[0]).astype(BF16) for x in xs]
    ks = [nn(x, w3[1]).astype(BF16) for x in xs]
    vts = [nt(wt3[2], x).astype(BF16) for x in xs]
    ss = [nt(k, nn(m_pick[n], q).astype(BF16) * m_side[...]) for q, k, (n, z) in zip(qs, ks, beside)]
    ps = []
    for score, (n, z) in zip(ss, beside):
        every = pl.ds(5 - 5 * n, WT, stride=6)
        table = jnp.concatenate([low_cols[z, every, :], high_cols[z, every, :][:, 0 : WT - 128]], axis=1).T
        table = jnp.where(label(row, z, bottom) != label(lane, z, bottom), OFF, table)
        e = jnp.exp(score * SCALE + table)
        ps.append((e * (1.0 / jnp.sum(e, axis=0, keepdims=True))).astype(BF16))
    fulls = [nn(vt, p).astype(BF16) * m_sidet[...] for vt, p in zip(vts, ps)]
    mxs = [nt(m_sfold[...], full).astype(BF16) for full in fulls]
    for t, mx, (n, z) in zip(ts, mxs, beside):
        att = nn(mx, wproj[...]).astype(BF16)
        there = nn(m_there[n], t.astype(BF16))
        side[n, z] = (there + att.astype(F32)).astype(BF16)

    for lev in range(4):
        z, li = LEVEL_AT[lev]
        src = jnp.concatenate([resw[z * 4 + win, li * 72 : li * 72 + 72] for win in range(4)], axis=0).astype(BF16)
        src = jnp.concatenate([src, side[0, z, li * 16 : li * 16 + 16], side[1, z, li * 16 : li * 16 + 16]], axis=0)
        got = nn(m_quad[...], src).astype(BF16)
        for k in range(4):
            resq[k, lev * 80 : lev * 80 + 80] = got[k * 80 : k * 80 + 80]

    src = []
    for lev in range(4):
        src += [cot[lev], jnp.concatenate([dn[lev, 144:192], dn[lev, 192:240]], axis=1)]
    for block in (rt_, dr_):
        src.append(jnp.concatenate([block[216:240], block[240:264]], axis=1))
    src = jnp.concatenate(src[:8] + [jnp.concatenate(src[8:], axis=0).astype(BF16)], axis=0)
    cotq[...] = nn(m_cot[...], src).astype(BF16)

    g2 = gain_two[...]
    inner = np.float32(np.sqrt(2 / np.pi))

    def feed(k, carry):
        res = resq[k].astype(F32)
        hat, _ = norm_parts(res)
        mi = (hat * g2).astype(BF16)
        mlpin[k] = mi
        pre = nn(mi, wfc1[...])
        sq = pre * pre
        t = jnp.tanh(pre * (inner + (inner * 0.044715) * sq))
        half = 0.5 + 0.5 * t
        full = pre * half
        a = full.astype(BF16)
        act[k] = a
        dgel[k] = half + full * (1.0 - half) * (2 * inner + (6 * inner * 0.044715) * sq)
        blk[k] = (res + nt(a, wfc2t[...])).astype(BF16)
        return carry

    lax.fori_loop(0, 4, feed, 0)

    total = 0.0
    for k in range(4):
        total = total + jnp.sum(blk[k].astype(F32), axis=-1, keepdims=True)
    mean = total * (1.0 / 768)
    total = 0.0
    for k in range(4):
        center = blk[k].astype(F32) - mean
        total = total + jnp.sum(center * center, axis=-1, keepdims=True)
    rstd = lax.rsqrt(total * (1.0 / 768) + EPS)
    cq = cotq[...]
    pair = lax.broadcasted_iota(jnp.int32, (320, MG), 0) % 80 % 13
    cq_own = jnp.where(pair < 12, cq.astype(F32), 0.0).astype(BF16)
    out = 0.0
    sum_a = 0.0
    sum_b = 0.0
    for k in range(4):
        gm = gain_merge[:, k * D : k * D + D]
        hat = (blk[k].astype(F32) - mean) * rstd
        mn = (hat * gm).astype(BF16)
        wm = wmerge[k * D : k * D + D]
        out = out + nn(mn, wm)
        gmerge = tn(mn, cq_own).astype(BF16)
        for t in range(3):
            at = t * 768 + k * D
            grads[1, at : at + D] = gmerge[:, t * 128 : t * 128 + 128]
        g = nt(cq, wm) * gm
        sum_a = sum_a + jnp.sum(g, axis=-1, keepdims=True)
        sum_b = sum_b + jnp.sum(g * hat, axis=-1, keepdims=True)
    merged[...] = out.astype(BF16)
    sum_a = sum_a * (1.0 / 768)
    sum_b = sum_b * (1.0 / 768)
    pair = lax.broadcasted_iota(jnp.int32, (320, D), 0) % 80 % 13
    fc1 = 0.0
    fc2 = 0.0
    for k in range(4):
        wm = wmerge[k * D : k * D + D]
        hat = (blk[k].astype(F32) - mean) * rstd
        g = nt(cq, wm) * gain_merge[:, k * D : k * D + D]
        d = rstd * (g - sum_a - hat * sum_b)
        d = jnp.where(pair == (0 if k % 2 == 0 else 12), 0.0, d)
        db = d.astype(BF16)
        dpre = (nn(db, wfc2t[...]) * dgel[k]).astype(BF16)
        fc2 = fc2 + tn(db, act[k])
        fc1 = fc1 + tn(mlpin[k], dpre)
        dmlp = nt(dpre, wfc1[...])
        hat2, rstd2 = norm_parts(resq[k].astype(F32))
        dresq[k] = (db.astype(F32) + norm_back(hat2, rstd2, g2, dmlp)).astype(BF16)
    for base, value in ((0, fc1.astype(BF16)), (1152, fc2.astype(BF16))):
        for t in range(6):
            grads[0, base + t * D : base + t * D + D] = value[:, t * 128 : t * 128 + 128]

    for lev in range(4):
        z, li = LEVEL_AT[lev]
        src = jnp.concatenate([dresq[k, lev * 80 : lev * 80 + 80] for k in range(4)], axis=0)
        got = nn(m_back[...], src)
        for win in range(4):
            resw[z * 4 + win, li * 72 : li * 72 + 72] = got[win * 72 : win * 72 + 72]
    dout[...] = resw[...].astype(BF16)
    grads[:, 2304:HALF] = jnp.zeros((2, HALF - 2304, 128), BF16)
    gproj = tn(mixed[...].reshape(8 * WT, D), dout[...].reshape(8 * WT, D)).astype(BF16)
    grads[0, 2304 : 2304 + D] = gproj[:, 0:128]
    grads[1, 2304 : 2304 + D, 0:64] = gproj[:, 128:192]
    core = core_ref[0, 0]
    stay[...] = grads[core]
    leave[...] = grads[1 - core]


def second_kernel(
    xn, prob, datt, wqkv, wproj, m_head, m_headt, m_fold,
    grads, dqkv,
    w3, wt3, gb,
):
    split_weights(wqkv, w3, wt3)
    gb[...] = jnp.zeros_like(gb)

    def backward(i, carry):
        ws = [i * GROUP + n for n in range(GROUP)]
        xs = [xn[w] for w in ws]
        ups = [datt[w] for w in ws]
        qs = [nn(x, w3[0]).astype(BF16) for x in xs]
        vs = [nn(x, w3[2]).astype(BF16) for x in xs]
        kts = [nt(wt3[1], x).astype(BF16) for x in xs]
        dms = [nt(up, wproj[...]).astype(BF16) for up in ups]
        dmbds = [jnp.concatenate([dm] * HEADS, axis=0) * m_head[...] for dm in dms]
        dps = [nt(v, dmbd) for v, dmbd in zip(vs, dmbds)]
        dsbs = []
        for w, dp in zip(ws, dps):
            p = prob[w].astype(F32)
            ds = p * (dp - jnp.sum(dp * p, axis=0, keepdims=True))
            gb[w // 4] += ds
            dsbs.append((ds * SCALE).astype(BF16))
        for w, dmbd in zip(ws, dmbds):
            dqkv[2, w] = nn(prob[w], dmbd).astype(BF16)
        qbds = [jnp.concatenate([q] * HEADS, axis=0) * m_head[...] for q in qs]
        for w, dsb, qbd in zip(ws, dsbs, qbds):
            dqkv[1, w] = nn(dsb, qbd).astype(BF16)
        fulls = [nn(kt, dsb).astype(BF16) * m_headt[...] for kt, dsb in zip(kts, dsbs)]
        for w, full in zip(ws, fulls):
            dqkv[0, w] = nt(m_fold[...], full).astype(BF16)
        return carry

    lax.fori_loop(0, 8 // GROUP, backward, 0)

    xs = xn[...].reshape(8 * WT, D)
    parts = [tn(xs, dqkv[part].reshape(8 * WT, D)) for part in range(3)]
    value = jnp.concatenate(parts, axis=1).astype(BF16)
    for t in range(4):
        grads[t * D : t * D + D] = value[:, t * 128 : t * 128 + 128]
    grads[768:960, 0:64] = value[:, 512:576]
    grads[768:960, 64:128] = jnp.zeros((D, 64), BF16)
    for z in range(2):
        total = gb[z].astype(BF16)
        for t in range(7):
            tile = total[:, t * 128 : min(t * 128 + 128, HQ)]
            if t == 6:
                tile = jnp.concatenate([tile, jnp.zeros((WT, 896 - HQ), BF16)], axis=1)
            at = BIAS_AT + (z * 7 + t) * WT
            grads[at : at + WT] = tile
    grads[BIAS_AT + 14 * WT :] = jnp.zeros((PEERS * SECOND - BIAS_AT - 14 * WT, 128), BF16)


def third_kernel(
    tok8, datt, dqkv, merged, gain_one, wqkv, m_out, m_merged,
    keep_t, keep_m, to_rt, to_dn, to_dr,
    gt,
):
    g1 = gain_one[...]
    ws = [wqkv[:, part * D : (part + 1) * D] for part in range(3)]
    for w in range(8):
        dnorm = (nt(dqkv[0, w], ws[0]) + nt(dqkv[1, w], ws[1]) + nt(dqkv[2, w], ws[2])).astype(BF16).astype(F32)
        hat, rstd = norm_parts(tok8[w].astype(F32))
        gt[w] = (datt[w].astype(F32) + norm_back(hat, rstd, g1, dnorm)).astype(BF16).astype(F32)

    for lev in range(4):
        z, li = LEVEL_AT[lev]
        src = jnp.concatenate([gt[z * 4 + win, li * 72 : li * 72 + 72] for win in range(4)], axis=0).astype(BF16)
        got = nn(m_out[...], src).astype(BF16)
        keep_t[lev] = got[0:144]
        to_dn[lev, 0:144] = got[144:288]
        to_rt[lev, 0:32] = got[288:320]
        to_dr[lev, 0:32] = got[320:352]
        got = nn(m_merged[...], merged[lev * 80 : lev * 80 + 80]).astype(BF16)
        keep_m[lev] = got[0:48]
        for half in range(2):
            part = got[:, half * D : half * D + D]
            to_dn[lev, 144 + 48 * half : 192 + 48 * half] = part[48:96]
            to_rt[lev, 32 + 16 * half : 48 + 16 * half] = part[96:112]
            to_dr[lev, 32 + 16 * half : 48 + 16 * half] = part[112:128]


def place_kernel(keep_t, keep_m, rt, dn, dr, m_place, m_pm, grad_tokens, merged):
    def halves(ref, lev, start, count):
        return jnp.concatenate([ref[lev, start : start + count], ref[lev, start + count : start + 2 * count]], axis=1)

    for lev in range(4):
        low = keep_t[lev].astype(F32) + nn(m_place[...], rt[lev, 0:32])
        top = dn[lev, 0:144].astype(F32) + nn(m_place[...], dr[lev, 0:32])
        grad_tokens[lev, 0:144] = top.astype(BF16)
        grad_tokens[lev, 144:288] = low.astype(BF16)
    src = [keep_m[lev] for lev in range(4)]
    src += [halves(dn, lev, 144, 48) for lev in range(4)]
    src += [halves(rt, lev, 32, 16) for lev in range(4)]
    src += [halves(dr, lev, 32, 16) for lev in range(4)]
    got = nn(m_pm[...], jnp.concatenate(src, axis=0)).astype(BF16)
    for i in range(72):
        merged[i] = got[4 * i : 4 * i + 4]


def add_kernel(is_weight, got, out, *, bands):
    count = got.shape[0]
    mine = got[0, 0:FIRST].astype(F32)
    for n in range(1, count):
        mine = mine + got[n, 0:FIRST].astype(F32)
    mine = mine.astype(BF16)
    total = 0.0
    parts = []
    for b in range(bands):
        part = got[b, FIRST:ROWS].astype(F32)
        for n in range(b + bands, count, bands):
            part = part + got[n, FIRST:ROWS].astype(F32)
        parts.append(part)
        total = total + part
    flag = is_weight[0, 0] > 0
    for b in range(bands):
        part = jnp.where(flag, total, parts[b]).astype(BF16)
        for n in range(b, count, bands):
            out[n, 0:FIRST] = mine
            out[n, FIRST:ROWS] = part


def pieces(start, count, size):
    while count:
        chunk, off = start // size, start % size
        take = min(count, size - off)
        yield chunk, off, take
        start, count = start + take, count - take


def bias_kernel(buf, gbias, *, scale):
    def rows(start, count):
        got = [buf[c, FIRST + off : FIRST + off + n].astype(F32) for c, off, n in pieces(start, count, SECOND)]
        return jnp.concatenate(got, axis=0)

    for z in range(2):
        for t in range(7):
            part = rows(BIAS_AT + (z * 7 + t) * WT, WT).T * scale
            end = min(t * 128 + 128, HQ)
            gbias[z, t * 128 : end] = part[0 : end - t * 128]


def final_kernel(core_ref, buf, oth, gqkv, gproj, gfc1, gfc2t, gmerge, *, scale):
    here = core_ref[0, 0]

    def first(half, start, count):
        got = []
        for c, off, n in pieces(start, count, FIRST):
            got.append(jnp.where(here == half, buf[c, off : off + n], oth[c, off : off + n]).astype(F32))
        return jnp.concatenate(got, axis=0) * scale

    def second(start, count):
        got = []
        for c, off, n in pieces(start, count, SECOND):
            at = FIRST + off
            got.append(buf[c, at : at + n].astype(F32) + oth[c, at : at + n].astype(F32))
        return jnp.concatenate(got, axis=0) * scale

    for t in range(6):
        gfc1[:, t * 128 : t * 128 + 128] = first(0, t * D, D)
        gfc2t[:, t * 128 : t * 128 + 128] = first(0, 1152 + t * D, D)
    for t in range(3):
        gmerge[:, t * 128 : t * 128 + 128] = first(1, t * 768, 768)
    gproj[:, 0:128] = first(0, 2304, D)
    gproj[:, 128:192] = first(1, 2304, D)[:, 0:64]
    for t in range(5):
        end = min(t * 128 + 128, 576)
        gqkv[:, t * 128 : end] = second(t * D, D)[:, 0 : end - t * 128]


def call(kernel, outs, scratch=(), flops=10**7, size=10**6, limit=16, **more):
    return pl.pallas_call(
        kernel,
        out_shape=outs,
        **more,
        scratch_shapes=list(scratch),
        compiler_params=pltpu.CompilerParams(vmem_limit_bytes=limit * 2**20),
        cost_estimate=pl.CostEstimate(flops=flops, bytes_accessed=size, transcendentals=0),
    )


def shape(*dims, kind=BF16):
    return jax.ShapeDtypeStruct(dims, kind)


def first_call():
    return call(
        first_kernel,
        (
            shape(HALF, 128),
            shape(HALF, 128),
            shape(320, MG),
            shape(8, WT, D),
            shape(8, WT, D),
            shape(8, WT, HQ),
            shape(8, WT, D),
        ),
        [
            pltpu.VMEM((2, HALF, 128), BF16),
            pltpu.VMEM((3, D, D), BF16),
            pltpu.VMEM((3, D, D), BF16),
            pltpu.VMEM((2, WT, HQ), F32),
            pltpu.VMEM((2, HQ, 128), F32),
            pltpu.VMEM((2, HQ, 128), F32),
            pltpu.VMEM((160, D), F32),
            pltpu.VMEM((8, WT, D), BF16),
            pltpu.VMEM((12, WT, D), F32),
            pltpu.VMEM((2, 2, 32, D), BF16),
            pltpu.VMEM((4, 320, D), BF16),
            pltpu.VMEM((4, 320, D), BF16),
            pltpu.VMEM((4, 320, FF), BF16),
            pltpu.VMEM((4, 320, FF), F32),
            pltpu.VMEM((4, 320, D), BF16),
            pltpu.VMEM((4, 320, D), BF16),
            pltpu.VMEM((8, WT, D), F32),
            pltpu.VMEM((320, MG), BF16),
        ],
        flops=2 * 10**10,
        size=10**7,
        limit=58,
    )


def second_call():
    return call(
        second_kernel,
        (shape(PEERS * SECOND, 128), shape(3, 8, WT, D)),
        [
            pltpu.VMEM((3, D, D), BF16),
            pltpu.VMEM((3, D, D), BF16),
            pltpu.VMEM((2, WT, HQ), F32),
        ],
        flops=10**10,
        size=10**7,
        limit=32,
    )


def third_call():
    return call(
        third_kernel,
        (shape(4, 144, D), shape(4, 48, MG), shape(4, 64, D), shape(4, 240, D), shape(4, 64, D)),
        [pltpu.VMEM((8, WT, D), F32)],
        flops=10**10,
        size=10**7,
    )


def body(tokens, gain_one, w_qkv, w_proj, bias_table, gain_two, w_fc1, w_fc2, gain_merge, w_merge, cotangent):
    lat_count = lax.axis_size(LAT)
    lon_count = lax.axis_size("lon")
    count = lat_count * lon_count
    peers = ("lon", "chip")
    bottom = (lax.axis_index(LAT) == lat_count - 1).astype(jnp.int32).reshape(1, 1)
    core = lax.axis_index("core").reshape(1, 1)
    flat = tokens.reshape(4, 288, D)

    def move(block, lon_step, lat_step):
        route = []
        for a in range(lon_count):
            for b in range(lat_count):
                to = (a + lon_step) % lon_count * lat_count + (b + lat_step) % lat_count
                route.append((a * lat_count + b, to))
        return lax.ppermute(block, ("lon",) + LAT, route)

    dn, rt, lf, dr, dl, cot = call(
        pack_kernel,
        (
            shape(4, 240, D),
            shape(272, D),
            shape(80, D),
            shape(272, D),
            shape(80, D),
            shape(4, 48, MG),
        ),
        [pltpu.VMEM((288, MG), F32), pltpu.VMEM((2, 272, D), F32), pltpu.VMEM((2, 80, D), F32)],
        limit=58,
    )(flat, cotangent.transpose(1, 2, 0, 3).reshape(72, 4, MG), pack_map(), pack_cot_map())
    dn = move(dn, 0, -1)
    rt = move(rt, -1, 0)
    lf = move(lf, 1, 0)
    dr = move(dr, -1, -1)
    dl = move(dl, 1, -1)

    head, headt, sidem, fold = head_mask(), head_mask().T, side_mask(), fold_map()
    g1 = gain_one.reshape(1, D)
    first, leave, merged, tok8, xn, prob, datt = first_call()(
        core, bottom, flat, dn, rt, lf, dr, dl, cot, bias_table.reshape(2, HQ, WT),
        g1, w_qkv, w_proj, gain_two.reshape(1, D), w_fc1, w_fc2.T, gain_merge.reshape(1, FF), w_merge,
        window_map(), cot_map(), quad_map(), back_map(), head, headt, fold, sidem, sidem.T, side_fold(),
        jnp.stack([side_pick(5, False), side_pick(0, False)]), jnp.stack([side_pick(5, True), side_pick(0, True)]),
    )
    arrived = lax.ppermute(leave, "core", [(0, 1), (1, 0)])
    second, dqkv = second_call()(xn, prob, datt, w_qkv, w_proj, head, headt, fold)
    arrived, second = lax.optimization_barrier((arrived, second))
    first = (first.astype(F32) + arrived.astype(F32)).astype(BF16).reshape(PEERS, FIRST, 128)
    grads = jnp.concatenate([first, second.reshape(PEERS, SECOND, 128)], axis=1)
    grads = lax.all_to_all(grads, peers, 0, 0)
    keep_t, keep_m, rt, dn, dr = third_call()(tok8, datt, dqkv, merged, g1, w_qkv, out_map(), merged_map())
    rt = move(rt, 1, 0)
    dn = move(dn, 0, 1)
    dr = move(dr, 1, 1)
    grads, rt, dn, dr = lax.optimization_barrier((grads, rt, dn, dr))
    place = lax.axis_index(peers)
    is_weight = (place < BIAS_AT // SECOND).astype(jnp.int32).reshape(1, 1)
    grads = call(
        functools.partial(add_kernel, bands=lax.axis_size("chip")), shape(PEERS, ROWS, 128), in_specs=[SCALAR, WHOLE]
    )(is_weight, grads)
    grads = lax.all_to_all(grads, peers, 0, 0)
    grad_tokens, merged = call(place_kernel, (shape(4, 288, D), shape(72, 4, MG)))(
        keep_t, keep_m, rt, dn, dr, place_map(), place_merged_map()
    )
    grads, grad_tokens, merged = lax.optimization_barrier((grads, grad_tokens, merged))
    other = lax.ppermute(grads, "core", [(0, 1), (1, 0)])
    gbias = call(
        functools.partial(bias_kernel, scale=WT * (4 * lon_count) ** (-0.5)), shape(2, HQ, WT, kind=F32)
    )(grads)
    gqkv, gproj, gfc1, gfc2t, gmerge = call(
        functools.partial(final_kernel, scale=(1152 * count) ** (-0.5)),
        (
            shape(D, 3 * D, kind=F32),
            shape(D, D, kind=F32),
            shape(D, FF, kind=F32),
            shape(D, FF, kind=F32),
            shape(FF, MG, kind=F32),
        ),
        in_specs=[SCALAR, WHOLE, WHOLE],
    )(core, grads, other)
    return (
        merged.reshape(6, 12, 4, MG).transpose(2, 0, 1, 3),
        grad_tokens.reshape(4, 12, 24, D),
        gqkv,
        gproj,
        gfc1,
        gfc2t.T,
        gmerge,
        gbias.reshape(1, 2, HEADS, WT, WT),
    )


def solution(mesh):
    lons, lats = mesh.devices.shape
    mesh = jax.sharding.Mesh(mesh.devices.reshape(lons, lats // 2, 2), ("lon",) + LAT)
    placed = (
        P(None, LAT, "lon", None),
        P(),
        P(),
        P(),
        P(LAT, None, None, None, None),
        P(),
        P(),
        P(),
        P(),
        P(),
        P(None, LAT, "lon", None),
    )
    return jax.shard_map(
        body,
        mesh=mesh,
        in_specs=placed,
        out_specs=(
            P(None, LAT, "lon", None),
            P(None, LAT, "lon", None),
            P(),
            P(),
            P(),
            P(),
            P(),
            P(LAT, None, None, None, None),
        ),
        check_vma=False,
    )
```

profile of v0, /device:TPU:1, one launch (start us, length us, event | category | flops | bytes accessed | tf_op | source)
XLA Modules:
  0.0 133.9 jit_solution(5506043032945367115)
XLA Ops:
  0.6 2.7 %shard_map.341 = (bf16[4,240,192]{2,1,0:T(8,128)(2,1)}, bf16[272,192]{1,0:T(8,128)(2,1)}, bf16[80,192]{1,0:T(8,128)(2,1)}, bf16[272,192]{1,0:T(8,128)(2,1)}, bf1...) custom-call(bf16[4,288,192]{2,1,0:T(8,128)(2,1)} %bitcast.24, bf16[72,4,384]{2,1,0:T(4,128)(2,1)} %bitcast.26, ...), custom_call_target="tpu_custom_call" | custom-call | flops 10000000 | bytes 1000000 | tf_op jit(solution)/shard_map/pallas_call | solution.py:701
  3.4 1.4 %collective-permute-start = (bf16[4,240,192]{2,1,0:T(8,128)(2,1)}, bf16[4,240,192]{2,1,0:T(8,128)(2,1)S(1)}, u32[]{:S(2)}, u32[]{:S(2)}) collective-permute-start(bf16[4,240,192]{2,1,0:T(8,128)(2,1)} %get-tuple-element.44), channel_id=1, source_target_pairs={{0,15},{1,0},{2,1},{3,2},{4,3},{5,4},{6,5},{7,6},{8,7},{9,8},{10,9... | collective-permute-start | bytes 1105928 | tf_op jit(solution)/shard_map/ppermute | solution.py:699
  4.8 5.9 %collective-permute-start.1 = (bf16[272,192]{1,0:T(8,128)(2,1)}, bf16[272,192]{1,0:T(8,128)(2,1)S(1)}, u32[]{:S(2)}, u32[]{:S(2)}) collective-permute-start(bf16[272,192]{1,0:T(8,128)(2,1)} %get-tuple-element.45), channel_id=1, source_target_pairs={{0,112},{1,113},{2,114},{3,115},{4,116},{5,117},{6,118},{7,119},{8... | collective-permute-start | bytes 313352 | tf_op jit(solution)/shard_map/ppermute | solution.py:699
  10.7 3.4 %collective-permute-start.3 = (bf16[272,192]{1,0:T(8,128)(2,1)}, bf16[272,192]{1,0:T(8,128)(2,1)S(1)}, u32[]{:S(2)}, u32[]{:S(2)}) collective-permute-start(bf16[272,192]{1,0:T(8,128)(2,1)} %get-tuple-element.47), channel_id=1, source_target_pairs={{0,127},{1,112},{2,113},{3,114},{4,115},{5,116},{6,117},{7,118},{8... | collective-permute-start | bytes 313352 | tf_op jit(solution)/shard_map/ppermute | solution.py:699
  14.1 3.2 %collective-permute-start.2 = (bf16[80,192]{1,0:T(8,128)(2,1)}, bf16[80,192]{1,0:T(8,128)(2,1)S(1)}, u32[]{:S(2)}, u32[]{:S(2)}) collective-permute-start(bf16[80,192]{1,0:T(8,128)(2,1)} %get-tuple-element.46), channel_id=1, source_target_pairs={{0,16},{1,17},{2,18},{3,19},{4,20},{5,21},{6,22},{7,23},{8,24},{9,... | collective-permute-start | bytes 92168 | tf_op jit(solution)/shard_map/ppermute | solution.py:699
  17.3 0.0 collective-permute-start.4
  17.3 1.3 reshape.72.gain_merge
  18.6 2.2 %collective-permute-done.2.lf = bf16[80,192]{1,0:T(8,128)(2,1)S(1)} collective-permute-done((bf16[80,192]{1,0:T(8,128)(2,1)}, bf16[80,192]{1,0:T(8,128)(2,1)S(1)}, u32[]{:S(2)}, u32[]{:S(2)}) %collective-permute-start.2) | collective-permute-done | bytes 30752 | tf_op jit(solution)/shard_map/ppermute | solution.py:699
  20.8 3.5 %collective-permute-done.4.dl = bf16[80,192]{1,0:T(8,128)(2,1)S(1)} collective-permute-done((bf16[80,192]{1,0:T(8,128)(2,1)}, bf16[80,192]{1,0:T(8,128)(2,1)S(1)}, u32[]{:S(2)}, u32[]{:S(2)}) %collective-permute-start.4) | collective-permute-done | bytes 30752 | tf_op jit(solution)/shard_map/ppermute | solution.py:699
  24.3 0.0 collective-permute-done.1.rt
  24.3 0.0 collective-permute-done.3.dr
  24.3 0.0 copy-start.21
  24.3 0.0 collective-permute-done.dn
  24.3 0.0 copy-start.19
  24.3 0.0 copy-done.22
  24.3 0.5 copy-done.23
  24.9 0.1 copy-done.20
  24.9 0.0 copy-done.21
  25.0 0.2 copy-done.19
  25.2 0.0 copy-start.8
  25.2 21.3 %shard_map.342 = (bf16[2560,128]{1,0:T(8,128)(2,1)}, bf16[2560,128]{1,0:T(8,128)(2,1)}, bf16[320,384]{1,0:T(8,128)(2,1)}, bf16[8,144,192]{2,1,0:T(8,128)(2,1)}, ...) custom-call(s32[1,1]{1,0:T(1,128)} %bitcast.1.core_ref, ...), custom_call_target="tpu_custom_call" | custom-call | flops 20000000000 | bytes 10000000 | tf_op jit(solution)/shard_map/pallas_call | solution.py:722
  46.5 0.3 collective-permute-start.5
  46.8 0.0 copy-done.2
  46.8 0.0 copy-done.3
  46.9 0.0 copy-done.5
  46.9 0.0 copy-done.6
  46.9 0.0 copy-done.8
  46.9 0.0 copy-start.10
  46.9 1.6 %copy-done.10 = bf16[8,144,864]{2,1,0:T(8,128)(2,1)S(1)} copy-done((bf16[8,144,864]{2,1,0:T(8,128)(2,1)S(1)}, bf16[8,144,864]{2,1,0:T(8,128)(2,1)}, u32[]{:S(2)}) %copy-start.10) | copy-done | bytes 1990680
  48.5 1.1 copy-done.13
  49.5 1.1 copy-done.15
  50.6 6.1 %shard_map.343 = (bf16[3072,128]{1,0:T(8,128)(2,1)S(1)}, bf16[3,8,144,192]{3,2,1,0:T(8,128)(2,1)S(1)}) custom-call(bf16[8,144,192]{2,1,0:T(8,128)(2,1)S(1)} %copy-done.15, bf16[8,144,864]{2,1,0:T(8,128)(2,1)S(1)} %copy-done.10, bf16[8,144,192]{2,1,0:T(8,128)(2,1)S(1)} %copy-done.13, bf16[192,576]{1,0:T(8,128)(2,1)S(1)} %copy-done.2, ...), custom_call_target="tpu_custom_call" | custom-call | flops 10000000000 | bytes 10000000 | tf_op jit(solution)/shard_map/pallas_call | solution.py:729
  56.7 0.0 copy-start.11
  56.7 0.0 collective-permute-done.5
  56.7 0.0 copy-done.18
  56.8 0.2 add_convert_fusion
  56.9 1.0 copy-done.11
  57.9 1.2 pad_maximum_fusion
  59.2 7.5 %all-to-all-start = ((bf16[64,88,128]{2,1,0:T(8,128)(2,1)}), bf16[64,88,128]{2,1,0:T(8,128)(2,1)S(1)}, u32[]{:S(2)}, u32[]{:S(2)}) async-start(bf16[64,88,128]{2,1,0:T(8,128)(2,1)} %pad_maximum_fusion), calls=%async_computation | async-start | bytes 2883584 | tf_op jit(solution)/shard_map/all_to_all | solution.py:733
  66.7 0.0 copy-done.4
  66.7 0.0 copy-done.7
  66.7 0.0 copy-done.9
  66.8 0.0 copy-start.12
  66.8 1.5 %copy-done.12 = bf16[3,8,144,192]{3,2,1,0:T(8,128)(2,1)S(1)} copy-done((bf16[3,8,144,192]{3,2,1,0:T(8,128)(2,1)S(1)}, bf16[3,8,144,192]{3,2,1,0:T(8,128)(2,1)}, u32[]{:S(2)}) %copy-start.12) | copy-done | bytes 1327128
  68.2 1.1 copy-done.14
  69.3 1.1 copy-done.16
  70.4 0.9 copy-done.17
  71.3 2.2 %shard_map.344 = (bf16[4,144,192]{2,1,0:T(8,128)(2,1)S(1)}, bf16[4,48,384]{2,1,0:T(8,128)(2,1)S(1)}, bf16[4,64,192]{2,1,0:T(8,128)(2,1)S(1)}, bf16[4,240,192]{2,1,0:T(8,128)(2,1)S(1)}, bf16[4,64,192]{2,1,0:T(8,128)(2,1)S(1)}) custom-call(bf16[8,144,192]{2,1,0:T(8,128)(2,1)S(1)} %copy-done.16, bf16[8,144,192]{2,1,0:T(8,128)(2,1)S(1)} %copy-done.14, ...), custom_call_target="tpu_custom_call" | custom-call | flops 10000000000 | bytes 10000000 | tf_op jit(solution)/shard_map/pallas_call | solution.py:734
  73.5 2.0 %collective-permute-start.7 = (bf16[4,240,192]{2,1,0:T(8,128)(2,1)S(1)}, bf16[4,240,192]{2,1,0:T(8,128)(2,1)S(1)}, u32[]{:S(2)}, u32[]{:S(2)}) collective-permute-start(bf16[4,240,192]{2,1,0:T(8,128)(2,1)S(1)} %get-tuple-element.62), channel_id=1, source_target_pairs={{0,1},{1,2},{2,3},{3,4},{4,5},{5,6},{6,7},{7,8},{8,9},{9,10},{10,1... | collective-permute-start | bytes 1105928 | tf_op jit(solution)/shard_map/ppermute | solution.py:699
  75.5 2.4 %collective-permute-start.6 = (bf16[4,64,192]{2,1,0:T(8,128)(2,1)S(1)}, bf16[4,64,192]{2,1,0:T(8,128)(2,1)S(1)}, u32[]{:S(2)}, u32[]{:S(2)}) collective-permute-start(bf16[4,64,192]{2,1,0:T(8,128)(2,1)S(1)} %get-tuple-element.61), channel_id=1, source_target_pairs={{0,16},{1,17},{2,18},{3,19},{4,20},{5,21},{6,22},{7,23},{8,24},{9,... | collective-permute-start | bytes 294920 | tf_op jit(solution)/shard_map/ppermute | solution.py:699
  77.9 1.3 collective-permute-start.8
  79.2 15.2 %collective-permute-done.6.rt = bf16[4,64,192]{2,1,0:T(8,128)(2,1)S(1)} collective-permute-done((bf16[4,64,192]{2,1,0:T(8,128)(2,1)S(1)}, bf16[4,64,192]{2,1,0:T(8,128)(2,1)S(1)}, u32[]{:S(2)}, u32[]{:S(2)}) %collective-permute-start.6) | collective-permute-done | bytes 98336 | tf_op jit(solution)/shard_map/ppermute | solution.py:699
  94.4 0.0 collective-permute-done.8.dr
  94.4 0.0 collective-permute-done.7.dn
  94.4 0.0 all-to-all-done.got
  94.4 1.4 %shard_map.345 = bf16[64,88,128]{2,1,0:T(8,128)(2,1)} custom-call(s32[1,1]{1,0:T(1,128)} %bitcast.is_weight, bf16[64,88,128]{2,1,0:T(8,128)(2,1)S(1)} %all-to-all-done.got), custom_call_target="tpu_custom_call" | custom-call | flops 10000000 | bytes 1000000 | tf_op jit(solution)/shard_map/pallas_call | solution.py:741
  95.8 9.3 %all-to-all-start.1 = ((bf16[64,88,128]{2,1,0:T(8,128)(2,1)}), bf16[64,88,128]{2,1,0:T(8,128)(2,1)S(1)}, u32[]{:S(2)}, u32[]{:S(2)}) async-start(bf16[64,88,128]{2,1,0:T(8,128)(2,1)} %shard_map.345), calls=%async_computation.1 | async-start | bytes 2883584 | tf_op jit(solution)/shard_map/all_to_all | solution.py:744
  105.1 0.0 copy-done
  105.1 1.2 shard_map.346
  106.3 20.5 %all-to-all-done.1.buf = bf16[64,88,128]{2,1,0:T(8,128)(2,1)S(1)} async-done(((bf16[64,88,128]{2,1,0:T(8,128)(2,1)}), bf16[64,88,128]{2,1,0:T(8,128)(2,1)S(1)}, u32[]{:S(2)}, u32[]{:S(2)}) %all-to-all-start.1) | async-done | bytes 1441824 | tf_op jit(solution)/shard_map/all_to_all | solution.py:744
  126.8 2.2 %collective-permute-start.9 = (bf16[64,88,128]{2,1,0:T(8,128)(2,1)S(1)}, bf16[64,88,128]{2,1,0:T(8,128)(2,1)S(1)}, u32[]{:S(2)}, u32[]{:S(2)}) collective-permute-start(bf16[64,88,128]{2,1,0:T(8,128)(2,1)S(1)} %all-to-all-done.1.buf), channel_id=1, source_target_pairs={{0,1},{1,0},{2,3},{3,2},{4,5},{5,4},{6,7},{7,6},{8,9},{9,8},{10,11... | collective-permute-start | bytes 4325384 | tf_op jit(solution)/shard_map/ppermute | solution.py:749
  129.0 1.5 %shard_map.348 = f32[2,864,144]{2,1,0:T(8,128)} custom-call(bf16[64,88,128]{2,1,0:T(8,128)(2,1)S(1)} %all-to-all-done.1.buf), custom_call_target="tpu_custom_call" | custom-call | flops 10000000 | bytes 1000000 | tf_op jit(solution)/shard_map/pallas_call | solution.py:750
  130.5 1.3 collective-permute-done.9.oth
  131.9 2.1 %shard_map.347 = (f32[192,576]{1,0:T(8,128)}, f32[192,192]{1,0:T(8,128)}, f32[192,768]{1,0:T(8,128)}, f32[192,768]{1,0:T(8,128)}, f32[768,384]{1,0:T(8,128)}) custom-call(s32[1,1]{1,0:T(1,128)} %bitcast.1.core_ref, bf16[64,88,128]{2,1,0:T(8,128)(2,1)S(1)} %all-to-all-done.1.buf, bf16[64,88,128]{2,1,0:T(8,128)(2,1)S(1)} %collective-permute-done.9.oth), custom_call_target="tpu_custom_call" | custom-call | flops 10000000 | bytes 1000000 | tf_op jit(solution)/shard_map/pallas_call | solution.py:753
  (19 shorter events, 0.0 us)
Async XLA Ops:
  3.4 20.9 %collective-permute-start = (bf16[4,240,192]{2,1,0:T(8,128)(2,1)}, bf16[4,240,192]{2,1,0:T(8,128)(2,1)S(1)}, u32[]{:S(2)}, u32[]{:S(2)}) collective-permute-start(bf16[4,240,192]{2,1,0:T(8,128)(2,1)} %get-tuple-element.44), channel_id=1, source_target_pairs={{0,15},{1,0},{2,1},{3,2},{4,3},{5,4},{6,5},{7,6},{8,7},{9,8},{10,9... | collective-permute-start | bytes 1105928 | tf_op jit(solution)/shard_map/ppermute | solution.py:699
  4.8 19.5 %collective-permute-start.1 = (bf16[272,192]{1,0:T(8,128)(2,1)}, bf16[272,192]{1,0:T(8,128)(2,1)S(1)}, u32[]{:S(2)}, u32[]{:S(2)}) collective-permute-start(bf16[272,192]{1,0:T(8,128)(2,1)} %get-tuple-element.45), channel_id=1, source_target_pairs={{0,112},{1,113},{2,114},{3,115},{4,116},{5,117},{6,118},{7,119},{8... | collective-permute-start | bytes 313352 | tf_op jit(solution)/shard_map/ppermute | solution.py:699
  10.7 13.6 %collective-permute-start.3 = (bf16[272,192]{1,0:T(8,128)(2,1)}, bf16[272,192]{1,0:T(8,128)(2,1)S(1)}, u32[]{:S(2)}, u32[]{:S(2)}) collective-permute-start(bf16[272,192]{1,0:T(8,128)(2,1)} %get-tuple-element.47), channel_id=1, source_target_pairs={{0,127},{1,112},{2,113},{3,114},{4,115},{5,116},{6,117},{7,118},{8... | collective-permute-start | bytes 313352 | tf_op jit(solution)/shard_map/ppermute | solution.py:699
  14.1 6.7 %collective-permute-start.2 = (bf16[80,192]{1,0:T(8,128)(2,1)}, bf16[80,192]{1,0:T(8,128)(2,1)S(1)}, u32[]{:S(2)}, u32[]{:S(2)}) collective-permute-start(bf16[80,192]{1,0:T(8,128)(2,1)} %get-tuple-element.46), channel_id=1, source_target_pairs={{0,16},{1,17},{2,18},{3,19},{4,20},{5,21},{6,22},{7,23},{8,24},{9,... | collective-permute-start | bytes 92168 | tf_op jit(solution)/shard_map/ppermute | solution.py:699
  17.3 7.0 %collective-permute-start.4 = (bf16[80,192]{1,0:T(8,128)(2,1)}, bf16[80,192]{1,0:T(8,128)(2,1)S(1)}, u32[]{:S(2)}, u32[]{:S(2)}) collective-permute-start(bf16[80,192]{1,0:T(8,128)(2,1)} %get-tuple-element.48), channel_id=1, source_target_pairs={{0,31},{1,16},{2,17},{3,18},{4,19},{5,20},{6,21},{7,22},{8,23},{9,... | collective-permute-start | bytes 92168 | tf_op jit(solution)/shard_map/ppermute | solution.py:699
  20.8 3.5 %copy-start.22 = (bf16[80,192]{1,0:T(8,128)(2,1)}, bf16[80,192]{1,0:T(8,128)(2,1)S(1)}, u32[]{:S(2)}) copy-start(bf16[80,192]{1,0:T(8,128)(2,1)S(1)} %collective-permute-done.2.lf) | copy-start | bytes 92164
  24.3 0.6 copy-start.23
  24.3 0.7 copy-start.20
  24.3 0.7 copy-start.21
  24.3 0.8 copy-start.19
  25.2 21.7 %copy-start.2 = (bf16[192,576]{1,0:T(8,128)(2,1)S(1)}, bf16[192,576]{1,0:T(8,128)(2,1)}, u32[]{:S(2)}) copy-start(bf16[192,576]{1,0:T(8,128)(2,1)} %wqkv.5) | copy-start | bytes 663556
  25.2 21.7 %copy-start.3 = (bf16[192,192]{1,0:T(8,128)(2,1)S(1)}, bf16[192,192]{1,0:T(8,128)(2,1)}, u32[]{:S(2)}) copy-start(bf16[192,192]{1,0:T(8,128)(2,1)} %wproj.3) | copy-start | bytes 221188
  25.2 21.7 %copy-start.5 = (bf16[864,192]{1,0:T(8,128)(2,1)S(1)}, bf16[864,192]{1,0:T(8,128)(2,1)}, u32[]{:S(2)}) copy-start(bf16[864,192]{1,0:T(8,128)(2,1)} %constant.58.clone.m_head) | copy-start | bytes 995332
  25.2 21.7 %copy-start.6 = (bf16[192,864]{1,0:T(8,128)(2,1)S(1)}, bf16[192,864]{1,0:T(8,128)(2,1)}, u32[]{:S(2)}) copy-start(bf16[192,864]{1,0:T(8,128)(2,1)} %constant.77.m_headt) | copy-start | bytes 995332
  25.2 21.7 %copy-start.8 = (bf16[144,864]{1,0:T(8,128)(2,1)S(1)}, bf16[144,864]{1,0:T(8,128)(2,1)}, u32[]{:S(2)}) copy-start(bf16[144,864]{1,0:T(8,128)(2,1)} %constant.60.clone.m_fold) | copy-start | bytes 746500
  46.5 10.2 %collective-permute-start.5 = (bf16[2560,128]{1,0:T(8,128)(2,1)}, bf16[2560,128]{1,0:T(8,128)(2,1)S(1)}, u32[]{:S(2)}, u32[]{:S(2)}) collective-permute-start(bf16[2560,128]{1,0:T(8,128)(2,1)} %get-tuple-element.51), channel_id=1, source_target_pairs={{0,1},{1,0},{2,3},{3,2},{4,5},{5,4},{6,7},{7,6},{8,9},{9,8},{10,11... | collective-permute-start | bytes 1966088 | tf_op jit(solution)/shard_map/ppermute | solution.py:728
  46.9 1.6 %copy-start.10 = (bf16[8,144,864]{2,1,0:T(8,128)(2,1)S(1)}, bf16[8,144,864]{2,1,0:T(8,128)(2,1)}, u32[]{:S(2)}) copy-start(bf16[8,144,864]{2,1,0:T(8,128)(2,1)} %get-tuple-element.53.prob) | copy-start | bytes 5971972
  48.5 1.1 copy-start.13
  49.5 1.1 copy-start.15
  50.6 6.2 %copy-start.18 = (bf16[2560,128]{1,0:T(8,128)(2,1)S(1)}, bf16[2560,128]{1,0:T(8,128)(2,1)}, u32[]{:S(2)}) copy-start(bf16[2560,128]{1,0:T(8,128)(2,1)} %get-tuple-element.50) | copy-start | bytes 1966084
  56.7 1.2 copy-start.11
  59.2 7.5 %copy-start.4 = (f32[192]{0:T(256)S(1)}, f32[192]{0:T(256)}, u32[]{:S(2)}) copy-start(f32[192]{0:T(256)} %param.31) | copy-start | bytes 2308
  59.2 7.6 %copy-start.7 = (bf16[352,288]{1,0:T(8,128)(2,1)S(1)}, bf16[352,288]{1,0:T(8,128)(2,1)}, u32[]{:S(2)}) copy-start(bf16[352,288]{1,0:T(8,128)(2,1)} %constant.70.clone.m_out) | copy-start | bytes 608260
  59.2 7.6 %copy-start.9 = (bf16[128,80]{1,0:T(8,128)(2,1)S(1)}, bf16[128,80]{1,0:T(8,128)(2,1)}, u32[]{:S(2)}) copy-start(bf16[128,80]{1,0:T(8,128)(2,1)} %constant.71.clone.m_merged) | copy-start | bytes 61444
  59.2 35.2 %all-to-all-start = ((bf16[64,88,128]{2,1,0:T(8,128)(2,1)}), bf16[64,88,128]{2,1,0:T(8,128)(2,1)S(1)}, u32[]{:S(2)}, u32[]{:S(2)}) async-start(bf16[64,88,128]{2,1,0:T(8,128)(2,1)} %pad_maximum_fusion), calls=%async_computation | async-start | bytes 2883584 | tf_op jit(solution)/shard_map/all_to_all | solution.py:733
  66.8 1.5 %copy-start.12 = (bf16[3,8,144,192]{3,2,1,0:T(8,128)(2,1)S(1)}, bf16[3,8,144,192]{3,2,1,0:T(8,128)(2,1)}, u32[]{:S(2)}) copy-start(bf16[3,8,144,192]{3,2,1,0:T(8,128)(2,1)} %copy-done.11) | copy-start | bytes 3981316
  68.2 1.1 copy-start.14
  69.3 1.1 copy-start.16
  70.4 0.9 copy-start.17
  73.5 20.9 %collective-permute-start.7 = (bf16[4,240,192]{2,1,0:T(8,128)(2,1)S(1)}, bf16[4,240,192]{2,1,0:T(8,128)(2,1)S(1)}, u32[]{:S(2)}, u32[]{:S(2)}) collective-permute-start(bf16[4,240,192]{2,1,0:T(8,128)(2,1)S(1)} %get-tuple-element.62), channel_id=1, source_target_pairs={{0,1},{1,2},{2,3},{3,4},{4,5},{5,6},{6,7},{7,8},{8,9},{9,10},{10,1... | collective-permute-start | bytes 1105928 | tf_op jit(solution)/shard_map/ppermute | solution.py:699
  75.5 18.9 %collective-permute-start.6 = (bf16[4,64,192]{2,1,0:T(8,128)(2,1)S(1)}, bf16[4,64,192]{2,1,0:T(8,128)(2,1)S(1)}, u32[]{:S(2)}, u32[]{:S(2)}) collective-permute-start(bf16[4,64,192]{2,1,0:T(8,128)(2,1)S(1)} %get-tuple-element.61), channel_id=1, source_target_pairs={{0,16},{1,17},{2,18},{3,19},{4,20},{5,21},{6,22},{7,23},{8,24},{9,... | collective-permute-start | bytes 294920 | tf_op jit(solution)/shard_map/ppermute | solution.py:699
  77.9 16.5 %collective-permute-start.8 = (bf16[4,64,192]{2,1,0:T(8,128)(2,1)S(1)}, bf16[4,64,192]{2,1,0:T(8,128)(2,1)S(1)}, u32[]{:S(2)}, u32[]{:S(2)}) collective-permute-start(bf16[4,64,192]{2,1,0:T(8,128)(2,1)S(1)} %get-tuple-element.63), channel_id=1, source_target_pairs={{0,17},{1,18},{2,19},{3,20},{4,21},{5,22},{6,23},{7,24},{8,25},{9,... | collective-permute-start | bytes 294920 | tf_op jit(solution)/shard_map/ppermute | solution.py:699
  95.8 9.3 %copy-start = (bf16[288,512]{1,0:T(8,128)(2,1)S(1)}, bf16[288,512]{1,0:T(8,128)(2,1)}, u32[]{:S(2)}) copy-start(bf16[288,512]{1,0:T(8,128)(2,1)} %constant.73.clone.m_pm) | copy-start | bytes 884740
  95.8 9.3 %copy-start.1 = (bf16[144,32]{1,0:T(8,128)(2,1)S(1)}, bf16[144,32]{1,0:T(8,128)(2,1)}, u32[]{:S(2)}) copy-start(bf16[144,32]{1,0:T(8,128)(2,1)} %constant.72.clone.m_place) | copy-start | bytes 27652
  95.8 31.0 %all-to-all-start.1 = ((bf16[64,88,128]{2,1,0:T(8,128)(2,1)}), bf16[64,88,128]{2,1,0:T(8,128)(2,1)S(1)}, u32[]{:S(2)}, u32[]{:S(2)}) async-start(bf16[64,88,128]{2,1,0:T(8,128)(2,1)} %shard_map.345), calls=%async_computation.1 | async-start | bytes 2883584 | tf_op jit(solution)/shard_map/all_to_all | solution.py:744
  126.8 5.1 %collective-permute-start.9 = (bf16[64,88,128]{2,1,0:T(8,128)(2,1)S(1)}, bf16[64,88,128]{2,1,0:T(8,128)(2,1)S(1)}, u32[]{:S(2)}, u32[]{:S(2)}) collective-permute-start(bf16[64,88,128]{2,1,0:T(8,128)(2,1)S(1)} %all-to-all-done.1.buf), channel_id=1, source_target_pairs={{0,1},{1,0},{2,3},{3,2},{4,5},{5,4},{6,7},{7,6},{8,9},{9,8},{10,11... | collective-permute-start | bytes 4325384 | tf_op jit(solution)/shard_map/ppermute | solution.py:749
where the time goes:
time: 135 us; the launch traced here: 134 us
  waiting for transfers between devices  42.7 us (32%)
  starting transfers between devices  38.9 us (29%)
  Pallas kernels  38.6 us (29%)
  local copies, waits for them, and re-layouts  11.4 us (8%)
  other arithmetic  1.42 us (1%)
    pallas_call x1, Pallas kernels, body(): first_call()  21.3 us
    ppermute x8, waiting for transfers between devices, move(): return lax.ppermute(block, ('lon',) + LAT, route)  20.9 us
    all_to_all x2, waiting for transfers between devices, body(): grads = lax.all_to_all(grads, peers, 0, 0)  20.5 us
    ppermute x8, starting transfers between devices, move(): return lax.ppermute(block, ('lon',) + LAT, route)  19.6 us
    all_to_all x2, starting transfers between devices, body(): grads = lax.all_to_all(grads, peers, 0, 0)  16.8 us
    unnamed x48, local copies, waits for them, and re-layouts  10.1 us
    pallas_call x1, Pallas kernels, body(): second_call()(xn, prob, datt, w_qkv, w_proj, head, headt, fold)  6.12 us
    pallas_call x1, Pallas kernels, body(): call(pack_kernel, (shape(4, 240, D), shape(272, D), shape(80, D), shape(2...  2.73 us
  transfers between devices with their start and end apart: 12, of which 5 were waited for; matrix products, arithmetic and copies ran while one was open for 1% of the time, Pallas kernels for 8%

commit v1 on v0

--- a/solution.py
+++ b/solution.py
@@ -157,10 +157,6 @@
     return one_hot((HQ, D), [(h * WT + q, h * HD + c) for h in range(HEADS) for q in range(WT) for c in range(HD)])
 
 
-def fold_map():
-    return one_hot((WT, HQ), [(q, h * WT + q) for h in range(HEADS) for q in range(WT)])
-
-
 def side_mask():
     return one_hot((WT, D), [(h * 24 + q, h * HD + c) for h in range(HEADS) for q in range(24) for c in range(HD)])
 
@@ -191,6 +187,11 @@
 
 def tn(a, b):
     return lax.dot_general(a, b, (((0,), (0,)), ((), ())), preferred_element_type=F32)
+
+
+def by_head(left, right):
+    parts = [nn(left[h * HD : h * HD + HD], right[:, h * WT : h * WT + WT]) for h in range(HEADS)]
+    return jnp.concatenate(parts, axis=0).T
 
 
 def norm_parts(values):
@@ -247,20 +248,50 @@
         wt3[part] = nt(eye, w).astype(BF16)
 
 
-def first_kernel(
-    core_ref, bottom_ref, own, dn, rt, lf, dr, dl, cot, bias, gain_one, wqkv, wproj, gain_two, wfc1, wfc2t, gain_merge, wmerge,
-    m_win, m_cot, m_quad, m_back, m_head, m_headt, m_fold, m_side, m_sidet, m_sfold, m_pick, m_there,
-    stay, leave, merged, tok8, xn, prob, dout,
-    grads, w3, wt3, bias_t, low_cols, high_cols, halo, mixed, tok, side, resq, mlpin, act, dgel, blk, dresq, resw, cotq,
-):
+def prepare_kernel(bottom_ref, wqkv, bias, w3, wt3, bias_t, side_t, low_cols, high_cols):
     split_weights(wqkv, w3, wt3)
     bottom = bottom_ref[0, 0] > 0
     lane = lax.broadcasted_iota(jnp.int32, (1, HQ), 1) % WT
     row = lax.broadcasted_iota(jnp.int32, (WT, 1), 0)
+    narrow = lax.broadcasted_iota(jnp.int32, (1, WT), 1) % 24
+    narrow = narrow // 12 * 72 + narrow % 12 * 6
     for z in range(2):
         bias_t[z] = jnp.where(label(row, z, bottom) != label(lane, z, bottom), OFF, bias[z].T)
-        low_cols[z] = bias[z, :, 0:128]
-        high_cols[z, :, 0 : WT - 128] = bias[z, :, 128:WT]
+        low_cols[...] = bias[z, :, 0:128]
+        high_cols[:, 0 : WT - 128] = bias[z, :, 128:WT]
+        for n in range(2):
+            every = pl.ds(5 - 5 * n, WT, stride=6)
+            table = jnp.concatenate([low_cols[every, :], high_cols[every, :][:, 0 : WT - 128]], axis=1).T
+            side_t[n, z] = jnp.where(label(row, z, bottom) != label(narrow, z, bottom), OFF, table)
+
+
+def staged(kernel, inputs, scalar_count=0):
+    def run(*refs):
+        scalars, refs = refs[:scalar_count], refs[scalar_count:]
+        fetched, rest = refs[:inputs], refs[inputs:]
+        places, sems, rest = rest[-inputs - 1 : -1], rest[-1], rest[: -inputs - 1]
+        copies = [pltpu.make_async_copy(a, b, sems.at[n]) for n, (a, b) in enumerate(zip(fetched, places))]
+        for copy in copies:
+            copy.start()
+
+        def arrive(first, last):
+            for copy in copies[first:last]:
+                copy.wait()
+
+        kernel(arrive, *scalars, *places, *rest)
+
+    return run
+
+
+def first_kernel(
+    arrive, core_ref, own, dn, rt, lf, dr, dl, m_win, gain_one,
+    w3, wt3, bias_t, side_t,
+    m_head, wproj, m_side, m_sidet, m_sfold, m_pick, m_there,
+    m_quad, cot, m_cot, gain_two, wfc1, wfc2t, gain_merge, wmerge, m_back,
+    stay, leave, merged, tok8_out, xn_out, prob_out, dout,
+    tok8, xn, prob, sent, grads, halo, mixed, tok, side, resq, mlpin, act, dgel, blk, dblk, dpres, dresq, resw, cotq,
+):
+    arrive(0, 8)
 
     halo[...] = jnp.zeros_like(halo)
     rt_, lf_, dr_, dl_ = (ref[...].astype(F32) for ref in (rt, lf, dr, dl))
@@ -276,6 +307,8 @@
             tok[z * 6 + win, li * 72 : li * 72 + 72] = got[win * 72 : win * 72 + 72]
 
     g1 = gain_one[...]
+
+    arrive(8, 19)
 
     def forward(i, carry):
         ws = [i * GROUP + n for n in range(GROUP)]
@@ -295,18 +328,20 @@
             p = (e * (1.0 / jnp.sum(e, axis=0, keepdims=True))).astype(BF16)
             prob[w] = p
             ps.append(p)
-        fulls = [nn(vt, p).astype(BF16) * m_headt[...] for vt, p in zip(vts, ps)]
-        mxs = [nt(m_fold[...], full).astype(BF16) for full in fulls]
+        mxs = [by_head(vt, p).astype(BF16) for vt, p in zip(vts, ps)]
         for w, t, mx in zip(ws, ts, mxs):
             mixed[w] = mx
             att = nn(mx, wproj[...]).astype(BF16)
             resw[w] = (t + att.astype(F32)).astype(BF16).astype(F32)
         return carry
 
-    lax.fori_loop(0, 8 // GROUP, forward, 0)
-
-    lane = lax.broadcasted_iota(jnp.int32, (1, WT), 1) % 24
-    lane = lane // 12 * 72 + lane % 12 * 6
+    forward(0, 0)
+    early = [
+        pltpu.make_async_copy(a, b, sent.at[n]) for n, (a, b) in enumerate(((tok8, tok8_out), (xn, xn_out), (prob, prob_out)))
+    ]
+    for copy in early:
+        copy.start()
+
     beside = [(n, z) for n in range(2) for z in range(2)]
     ts = [tok[z * 6 + 5 * n] for n, z in beside]
     xs = [(norm_parts(t)[0] * g1).astype(BF16) for t in ts]
@@ -316,10 +351,7 @@
     ss = [nt(k, nn(m_pick[n], q).astype(BF16) * m_side[...]) for q, k, (n, z) in zip(qs, ks, beside)]
     ps = []
     for score, (n, z) in zip(ss, beside):
-        every = pl.ds(5 - 5 * n, WT, stride=6)
-        table = jnp.concatenate([low_cols[z, every, :], high_cols[z, every, :][:, 0 : WT - 128]], axis=1).T
-        table = jnp.where(label(row, z, bottom) != label(lane, z, bottom), OFF, table)
-        e = jnp.exp(score * SCALE + table)
+        e = jnp.exp(score * SCALE + side_t[n, z])
         ps.append((e * (1.0 / jnp.sum(e, axis=0, keepdims=True))).astype(BF16))
     fulls = [nn(vt, p).astype(BF16) * m_sidet[...] for vt, p in zip(vts, ps)]
     mxs = [nt(m_sfold[...], full).astype(BF16) for full in fulls]
@@ -328,6 +360,8 @@
         there = nn(m_there[n], t.astype(BF16))
         side[n, z] = (there + att.astype(F32)).astype(BF16)
 
+    arrive(19, 28)
+
     for lev in range(4):
         z, li = LEVEL_AT[lev]
         src = jnp.concatenate([resw[z * 4 + win, li * 72 : li * 72 + 72] for win in range(4)], axis=0).astype(BF16)
@@ -347,7 +381,7 @@
     g2 = gain_two[...]
     inner = np.float32(np.sqrt(2 / np.pi))
 
-    def feed(k, carry):
+    def feed(k):
         res = resq[k].astype(F32)
         hat, _ = norm_parts(res)
         mi = (hat * g2).astype(BF16)
@@ -361,9 +395,9 @@
         act[k] = a
         dgel[k] = half + full * (1.0 - half) * (2 * inner + (6 * inner * 0.044715) * sq)
         blk[k] = (res + nt(a, wfc2t[...])).astype(BF16)
-        return carry
-
-    lax.fori_loop(0, 4, feed, 0)
+
+    for k in range(4):
+        feed(k)
 
     total = 0.0
     for k in range(4):
@@ -380,6 +414,7 @@
     out = 0.0
     sum_a = 0.0
     sum_b = 0.0
+    hats, gs = [], []
     for k in range(4):
         gm = gain_merge[:, k * D : k * D + D]
         hat = (blk[k].astype(F32) - mean) * rstd
@@ -391,27 +426,26 @@
             at = t * 768 + k * D
             grads[1, at : at + D] = gmerge[:, t * 128 : t * 128 + 128]
         g = nt(cq, wm) * gm
+        hats.append(hat)
+        gs.append(g)
         sum_a = sum_a + jnp.sum(g, axis=-1, keepdims=True)
         sum_b = sum_b + jnp.sum(g * hat, axis=-1, keepdims=True)
     merged[...] = out.astype(BF16)
     sum_a = sum_a * (1.0 / 768)
     sum_b = sum_b * (1.0 / 768)
     pair = lax.broadcasted_iota(jnp.int32, (320, D), 0) % 80 % 13
-    fc1 = 0.0
-    fc2 = 0.0
     for k in range(4):
-        wm = wmerge[k * D : k * D + D]
-        hat = (blk[k].astype(F32) - mean) * rstd
-        g = nt(cq, wm) * gain_merge[:, k * D : k * D + D]
-        d = rstd * (g - sum_a - hat * sum_b)
+        d = rstd * (gs[k] - sum_a - hats[k] * sum_b)
         d = jnp.where(pair == (0 if k % 2 == 0 else 12), 0.0, d)
         db = d.astype(BF16)
         dpre = (nn(db, wfc2t[...]) * dgel[k]).astype(BF16)
-        fc2 = fc2 + tn(db, act[k])
-        fc1 = fc1 + tn(mlpin[k], dpre)
+        dblk[k] = db
+        dpres[k] = dpre
         dmlp = nt(dpre, wfc1[...])
         hat2, rstd2 = norm_parts(resq[k].astype(F32))
         dresq[k] = (db.astype(F32) + norm_back(hat2, rstd2, g2, dmlp)).astype(BF16)
+    fc1 = tn(mlpin[...].reshape(1280, D), dpres[...].reshape(1280, FF))
+    fc2 = tn(dblk[...].reshape(1280, D), act[...].reshape(1280, FF))
     for base, value in ((0, fc1.astype(BF16)), (1152, fc2.astype(BF16))):
         for t in range(6):
             grads[0, base + t * D : base + t * D + D] = value[:, t * 128 : t * 128 + 128]
@@ -430,15 +464,17 @@
     core = core_ref[0, 0]
     stay[...] = grads[core]
     leave[...] = grads[1 - core]
+    for copy in early:
+        copy.wait()
 
 
 def second_kernel(
-    xn, prob, datt, wqkv, wproj, m_head, m_headt, m_fold,
+    arrive, w3, wt3, wproj, xn, datt, m_head, prob,
     grads, dqkv,
-    w3, wt3, gb,
+    gb,
 ):
-    split_weights(wqkv, w3, wt3)
     gb[...] = jnp.zeros_like(gb)
+    arrive(0, 6)
 
     def backward(i, carry):
         ws = [i * GROUP + n for n in range(GROUP)]
@@ -450,6 +486,7 @@
         dms = [nt(up, wproj[...]).astype(BF16) for up in ups]
         dmbds = [jnp.concatenate([dm] * HEADS, axis=0) * m_head[...] for dm in dms]
         dps = [nt(v, dmbd) for v, dmbd in zip(vs, dmbds)]
+        arrive(6, 7)
         dsbs = []
         for w, dp in zip(ws, dps):
             p = prob[w].astype(F32)
@@ -461,12 +498,11 @@
         qbds = [jnp.concatenate([q] * HEADS, axis=0) * m_head[...] for q in qs]
         for w, dsb, qbd in zip(ws, dsbs, qbds):
             dqkv[1, w] = nn(dsb, qbd).astype(BF16)
-        fulls = [nn(kt, dsb).astype(BF16) * m_headt[...] for kt, dsb in zip(kts, dsbs)]
-        for w, full in zip(ws, fulls):
-            dqkv[0, w] = nt(m_fold[...], full).astype(BF16)
+        for w, kt, dsb in zip(ws, kts, dsbs):
+            dqkv[0, w] = by_head(kt, dsb).astype(BF16)
         return carry
 
-    lax.fori_loop(0, 8 // GROUP, backward, 0)
+    backward(0, 0)
 
     xs = xn[...].reshape(8 * WT, D)
     parts = [tn(xs, dqkv[part].reshape(8 * WT, D)) for part in range(3)]
@@ -619,8 +655,40 @@
 
 
 def first_call():
+    held = pl.BlockSpec(memory_space=pltpu.HBM)
+    operands = [
+        shape(4, 288, D),
+        shape(4, 240, D),
+        shape(272, D),
+        shape(80, D),
+        shape(272, D),
+        shape(80, D),
+        shape(432, 448),
+        shape(1, D, kind=F32),
+        shape(3, D, D),
+        shape(3, D, D),
+        shape(2, WT, HQ, kind=F32),
+        shape(2, 2, WT, WT, kind=F32),
+        shape(HQ, D),
+        shape(D, D),
+        shape(WT, D),
+        shape(D, WT),
+        shape(32, WT),
+        shape(2, WT, WT),
+        shape(2, 32, WT),
+        shape(320, 320),
+        shape(4, 48, MG),
+        shape(320, 432),
+        shape(1, D, kind=F32),
+        shape(D, FF),
+        shape(D, FF),
+        shape(1, FF, kind=F32),
+        shape(FF, MG),
+        shape(288, 320),
+    ]
+    count = len(operands)
     return call(
-        first_kernel,
+        staged(first_kernel, count, 1),
         (
             shape(HALF, 128),
             shape(HALF, 128),
@@ -631,12 +699,11 @@
             shape(8, WT, D),
         ),
         [
+            pltpu.VMEM((8, WT, D), BF16),
+            pltpu.VMEM((8, WT, D), BF16),
+            pltpu.VMEM((8, WT, HQ), BF16),
+            pltpu.SemaphoreType.DMA((3,)),
             pltpu.VMEM((2, HALF, 128), BF16),
-            pltpu.VMEM((3, D, D), BF16),
-            pltpu.VMEM((3, D, D), BF16),
-            pltpu.VMEM((2, WT, HQ), F32),
-            pltpu.VMEM((2, HQ, 128), F32),
-            pltpu.VMEM((2, HQ, 128), F32),
             pltpu.VMEM((160, D), F32),
             pltpu.VMEM((8, WT, D), BF16),
             pltpu.VMEM((12, WT, D), F32),
@@ -647,27 +714,44 @@
             pltpu.VMEM((4, 320, FF), F32),
             pltpu.VMEM((4, 320, D), BF16),
             pltpu.VMEM((4, 320, D), BF16),
+            pltpu.VMEM((4, 320, FF), BF16),
+            pltpu.VMEM((4, 320, D), BF16),
             pltpu.VMEM((8, WT, D), F32),
             pltpu.VMEM((320, MG), BF16),
-        ],
+        ]
+        + [pltpu.VMEM(op.shape, op.dtype) for op in operands]
+        + [pltpu.SemaphoreType.DMA((count,))],
         flops=2 * 10**10,
         size=10**7,
         limit=58,
+        in_specs=[SCALAR] + [held] * count,
+        out_specs=(WHOLE, WHOLE, WHOLE, held, held, held, WHOLE),
     )
 
 
 def second_call():
+    operands = [
+        shape(3, D, D),
+        shape(3, D, D),
+        shape(D, D),
+        shape(8, WT, D),
+        shape(8, WT, D),
+        shape(HQ, D),
+        shape(8, WT, HQ),
+    ]
+    count = len(operands)
     return call(
-        second_kernel,
+        staged(second_kernel, count),
         (shape(PEERS * SECOND, 128), shape(3, 8, WT, D)),
         [
-            pltpu.VMEM((3, D, D), BF16),
-            pltpu.VMEM((3, D, D), BF16),
             pltpu.VMEM((2, WT, HQ), F32),
-        ],
+        ]
+        + [pltpu.VMEM(op.shape, op.dtype) for op in operands]
+        + [pltpu.SemaphoreType.DMA((count,))],
         flops=10**10,
         size=10**7,
-        limit=32,
+        limit=58,
+        in_specs=[pl.BlockSpec(memory_space=pltpu.HBM)] * count,
     )
 
 
@@ -678,6 +762,7 @@
         [pltpu.VMEM((8, WT, D), F32)],
         flops=10**10,
         size=10**7,
+        limit=58,
     )
 
 
@@ -717,16 +802,23 @@
     dr = move(dr, -1, -1)
     dl = move(dl, 1, -1)
 
-    head, headt, sidem, fold = head_mask(), head_mask().T, side_mask(), fold_map()
+    head, sidem = head_mask(), side_mask()
     g1 = gain_one.reshape(1, D)
+    w3, wt3, bias_t, side_t = call(
+        prepare_kernel,
+        (shape(3, D, D), shape(3, D, D), shape(2, WT, HQ, kind=F32), shape(2, 2, WT, WT, kind=F32)),
+        [pltpu.VMEM((HQ, 128), F32), pltpu.VMEM((HQ, 128), F32)],
+        limit=58,
+        in_specs=[SCALAR, WHOLE, WHOLE],
+    )(bottom, w_qkv, bias_table.reshape(2, HQ, WT))
     first, leave, merged, tok8, xn, prob, datt = first_call()(
-        core, bottom, flat, dn, rt, lf, dr, dl, cot, bias_table.reshape(2, HQ, WT),
-        g1, w_qkv, w_proj, gain_two.reshape(1, D), w_fc1, w_fc2.T, gain_merge.reshape(1, FF), w_merge,
-        window_map(), cot_map(), quad_map(), back_map(), head, headt, fold, sidem, sidem.T, side_fold(),
+        core, flat, dn, rt, lf, dr, dl, window_map(), g1, w3, wt3, bias_t, side_t,
+        head, w_proj, sidem, sidem.T, side_fold(),
         jnp.stack([side_pick(5, False), side_pick(0, False)]), jnp.stack([side_pick(5, True), side_pick(0, True)]),
+        quad_map(), cot, cot_map(), gain_two.reshape(1, D), w_fc1, w_fc2.T, gain_merge.reshape(1, FF), w_merge, back_map(),
     )
     arrived = lax.ppermute(leave, "core", [(0, 1), (1, 0)])
-    second, dqkv = second_call()(xn, prob, datt, w_qkv, w_proj, head, headt, fold)
+    second, dqkv = second_call()(w3, wt3, w_proj, xn, datt, head, prob)
     arrived, second = lax.optimization_barrier((arrived, second))
     first = (first.astype(F32) + arrived.astype(F32)).astype(BF16).reshape(PEERS, FIRST, 128)
     grads = jnp.concatenate([first, second.reshape(PEERS, SECOND, 128)], axis=1)

time: 135 us -> 127 us (0.941)
  local copies, waits for them, and re-layouts: 11.4 us -> 3.06 us
  Pallas kernels: 38.6 us -> 42.2 us
  waiting for transfers between devices: 42.7 us -> 40.3 us
    unnamed x48 -> x22, local copies, waits for them, and re-layouts: 10.1 us -> 1.78 us
    pallas_call x1 -> x2, Pallas kernels: 6.12 us -> 11.8 us  [the longest x1 8.18 us: body(): second, dqkv = second_call()(w3, wt3, w_proj, xn, datt, head, prob)]
    pallas_call x1, Pallas kernels: 21.3 us -> 16.3 us  [body(): first_call()]
    pallas_call x1, Pallas kernels: 2.23 us -> 5.14 us  [body(): third_call()(tok8, datt, dqkv, merged, g1, w_qkv, out_map(), merged_map())]
    ppermute x8, waiting for transfers between devices: 20.9 us -> 18.6 us  [move(): return lax.ppermute(block, ('lon',) + LAT, route)]
  transfers between devices with their start and end apart: 12 -> 12, of which waited for: 5 -> 4; matrix products, arithmetic and copies ran while one was open for 1% -> 1% of each run, Pallas kernels for 8% -> 16%
where the time goes in v1:
time: 127 us
  Pallas kernels  42.2 us (33%)
  waiting for transfers between devices  40.3 us (32%)
  starting transfers between devices  39 us (31%)
  local copies, waits for them, and re-layouts  3.06 us (2%)
  other arithmetic  1.4 us (1%)
    all_to_all x2, waiting for transfers between devices, body(): grads = lax.all_to_all(grads, peers, 0, 0)  20.5 us
    ppermute x8, starting transfers between devices, move(): return lax.ppermute(block, ('lon',) + LAT, route)  19.5 us
    ppermute x8, waiting for transfers between devices, move(): return lax.ppermute(block, ('lon',) + LAT, route)  18.6 us
    all_to_all x2, starting transfers between devices, body(): grads = lax.all_to_all(grads, peers, 0, 0)  17.1 us
    pallas_call x1, Pallas kernels, body(): first_call()  16.3 us
    pallas_call x1, Pallas kernels, body(): second, dqkv = second_call()(w3, wt3, w_proj, xn, datt, head, prob)  8.18 us
    pallas_call x1, Pallas kernels, body(): third_call()(tok8, datt, dqkv, merged, g1, w_qkv, out_map(), merged_map())  5.14 us
    pallas_call x1, Pallas kernels, body(): call(prepare_kernel, (shape(3, D, D), shape(3, D, D), shape(2, WT, HQ, ki...  3.67 us
  transfers between devices with their start and end apart: 12, of which 4 were waited for; matrix products, arithmetic and copies ran while one was open for 1% of the time, Pallas kernels for 16%

profile of v1, /device:TPU:1, one launch (start us, length us, event | category | flops | bytes accessed | tf_op | source)
XLA Modules:
  0.0 126.8 jit_solution(7804937546756591110)
XLA Ops:
  0.6 2.7 %shard_map.323 = (bf16[4,240,192]{2,1,0:T(8,128)(2,1)}, bf16[272,192]{1,0:T(8,128)(2,1)}, bf16[80,192]{1,0:T(8,128)(2,1)}, bf16[272,192]{1,0:T(8,128)(2,1)}, bf1...) custom-call(bf16[4,288,192]{2,1,0:T(8,128)(2,1)} %bitcast.23, bf16[72,4,384]{2,1,0:T(4,128)(2,1)} %bitcast.25, ...), custom_call_target="tpu_custom_call" | custom-call | flops 10000000 | bytes 1000000 | tf_op jit(solution)/shard_map/pallas_call | solution.py:786
  3.4 1.4 %collective-permute-start = (bf16[4,240,192]{2,1,0:T(8,128)(2,1)}, bf16[4,240,192]{2,1,0:T(8,128)(2,1)S(1)}, u32[]{:S(2)}, u32[]{:S(2)}) collective-permute-start(bf16[4,240,192]{2,1,0:T(8,128)(2,1)} %get-tuple-element.48), channel_id=1, source_target_pairs={{0,15},{1,0},{2,1},{3,2},{4,3},{5,4},{6,5},{7,6},{8,7},{9,8},{10,9... | collective-permute-start | bytes 1105928 | tf_op jit(solution)/shard_map/ppermute | solution.py:784
  4.8 5.9 %collective-permute-start.1 = (bf16[272,192]{1,0:T(8,128)(2,1)}, bf16[272,192]{1,0:T(8,128)(2,1)S(1)}, u32[]{:S(2)}, u32[]{:S(2)}) collective-permute-start(bf16[272,192]{1,0:T(8,128)(2,1)} %get-tuple-element.49), channel_id=1, source_target_pairs={{0,112},{1,113},{2,114},{3,115},{4,116},{5,117},{6,118},{7,119},{8... | collective-permute-start | bytes 313352 | tf_op jit(solution)/shard_map/ppermute | solution.py:784
  10.7 3.4 %collective-permute-start.3 = (bf16[272,192]{1,0:T(8,128)(2,1)}, bf16[272,192]{1,0:T(8,128)(2,1)S(1)}, u32[]{:S(2)}, u32[]{:S(2)}) collective-permute-start(bf16[272,192]{1,0:T(8,128)(2,1)} %get-tuple-element.51), channel_id=1, source_target_pairs={{0,127},{1,112},{2,113},{3,114},{4,115},{5,116},{6,117},{7,118},{8... | collective-permute-start | bytes 313352 | tf_op jit(solution)/shard_map/ppermute | solution.py:784
  14.1 3.2 %collective-permute-start.2 = (bf16[80,192]{1,0:T(8,128)(2,1)}, bf16[80,192]{1,0:T(8,128)(2,1)S(1)}, u32[]{:S(2)}, u32[]{:S(2)}) collective-permute-start(bf16[80,192]{1,0:T(8,128)(2,1)} %get-tuple-element.50), channel_id=1, source_target_pairs={{0,16},{1,17},{2,18},{3,19},{4,20},{5,21},{6,22},{7,23},{8,24},{9,... | collective-permute-start | bytes 92168 | tf_op jit(solution)/shard_map/ppermute | solution.py:784
  17.3 0.0 collective-permute-start.4
  17.3 1.3 %reshape.72.refs_26_ = f32[1,768]{1,0:T(1,128)} reshape(f32[768]{0:T(1024)} %param.36) | data formatting | bytes 6144 | tf_op jit(solution)/shard_map/reshape | solution.py:818
  18.6 3.7 %shard_map.324 = (bf16[3,192,192]{2,1,0:T(8,128)(2,1)}, bf16[3,192,192]{2,1,0:T(8,128)(2,1)}, f32[2,144,864]{2,1,0:T(8,128)}, f32[2,2,144,144]{3,2,1,0:T(8,128)}) custom-call(s32[1,1]{1,0:T(1,128)} %bitcast.6.bottom_ref, bf16[192,576]{1,0:T(8,128)(2,1)} %wqkv.3, f32[2,864,144]{2,1,0:T(8,128)} %bitcast.21), custom_call_target="tpu_custom_call" | custom-call | flops 10000000 | bytes 1000000 | tf_op jit(solution)/shard_map/pallas_call | solution.py:807
  22.3 0.0 collective-permute-done.2.refs_4_
  22.3 0.0 copy-start.9
  22.3 2.0 %collective-permute-done.4.refs_6_ = bf16[80,192]{1,0:T(8,128)(2,1)S(1)} collective-permute-done((bf16[80,192]{1,0:T(8,128)(2,1)}, bf16[80,192]{1,0:T(8,128)(2,1)S(1)}, u32[]{:S(2)}, u32[]{:S(2)}) %collective-permute-start.4) | collective-permute-done | bytes 30752 | tf_op jit(solution)/shard_map/ppermute | solution.py:784
  24.3 0.0 copy-start.10
  24.3 0.0 collective-permute-done.1.refs_3_
  24.3 0.0 copy-start.7
  24.3 0.0 collective-permute-done.3.refs_5_
  24.3 0.0 copy-start.8
  24.3 0.0 collective-permute-done.refs_2_
  24.3 0.0 copy-start.6
  24.3 0.0 copy-done.9
  24.3 0.6 copy-done.10
  24.9 0.1 copy-done.7
  24.9 0.0 copy-done.8
  25.0 0.2 copy-done.6
  25.2 16.3 %shard_map.325 = (bf16[2560,128]{1,0:T(8,128)(2,1)}, bf16[2560,128]{1,0:T(8,128)(2,1)}, bf16[320,384]{1,0:T(8,128)(2,1)}, bf16[8,144,192]{2,1,0:T(8,128)(2,1)}, ...) custom-call(s32[1,1]{1,0:T(1,128)} %bitcast.1.refs_0_.core_ref, ...), custom_call_target="tpu_custom_call" | custom-call | flops 20000000000 | bytes 10000000 | tf_op jit(solution)/shard_map/pallas_call | solution.py:814
  41.5 0.1 collective-permute-start.5
  41.6 0.0 copy-start.5
  41.6 8.2 %shard_map.326 = (bf16[3072,128]{1,0:T(8,128)(2,1)}, bf16[3,8,144,192]{3,2,1,0:T(8,128)(2,1)}) custom-call(bf16[3,192,192]{2,1,0:T(8,128)(2,1)} %get-tuple-element.53.refs_9_.refs_0_, bf16[3,192,192]{2,1,0:T(8,128)(2,1)} %get-tuple-element.54.refs_10_.refs_1_, bf16[192,192]{1,0:T(8,128)(2,1)} %refs_2_.1, bf16[8,144,192]{2,1,0:T(8,128)(2,1)} %get-tuple-element.60.refs_3_, ...), custom_call_target="tpu_custom_call" | custom-call | flops 10000000000 | bytes 10000000 | tf_op jit(solution)/shard_map/pallas_call | solution.py:821
  49.8 0.0 copy-start.4
  49.8 0.0 collective-permute-done.5
  49.8 0.0 copy-done.5
  49.8 0.2 add_convert_fusion
  50.0 0.9 copy-done.4
  50.9 1.2 pad_maximum_fusion
  52.1 7.4 %all-to-all-start = ((bf16[64,88,128]{2,1,0:T(8,128)(2,1)}), bf16[64,88,128]{2,1,0:T(8,128)(2,1)S(1)}, u32[]{:S(2)}, u32[]{:S(2)}) async-start(bf16[64,88,128]{2,1,0:T(8,128)(2,1)} %pad_maximum_fusion), calls=%async_computation | async-start | bytes 2883584 | tf_op jit(solution)/shard_map/all_to_all | solution.py:825
  59.5 5.1 %shard_map.327 = (bf16[4,144,192]{2,1,0:T(8,128)(2,1)}, bf16[4,48,384]{2,1,0:T(8,128)(2,1)}, bf16[4,64,192]{2,1,0:T(8,128)(2,1)}, bf16[4,240,192]{2,1,0:T(8,128)(2,1)}, bf16[4,64,192]{2,1,0:T(8,128)(2,1)}) custom-call(bf16[8,144,192]{2,1,0:T(8,128)(2,1)} %get-tuple-element.66.tok8, bf16[8,144,192]{2,1,0:T(8,128)(2,1)} %get-tuple-element.61.refs_4_.datt, ...), custom_call_target="tpu_custom_call" | custom-call | flops 10000000000 | bytes 10000000 | tf_op jit(solution)/shard_map/pallas_call | solution.py:826
  64.7 1.9 %collective-permute-start.7 = (bf16[4,240,192]{2,1,0:T(8,128)(2,1)}, bf16[4,240,192]{2,1,0:T(8,128)(2,1)S(1)}, u32[]{:S(2)}, u32[]{:S(2)}) collective-permute-start(bf16[4,240,192]{2,1,0:T(8,128)(2,1)} %get-tuple-element.70), channel_id=1, source_target_pairs={{0,1},{1,2},{2,3},{3,4},{4,5},{5,6},{6,7},{7,8},{8,9},{9,10},{10,1... | collective-permute-start | bytes 1105928 | tf_op jit(solution)/shard_map/ppermute | solution.py:784
  66.6 2.4 %collective-permute-start.6 = (bf16[4,64,192]{2,1,0:T(8,128)(2,1)}, bf16[4,64,192]{2,1,0:T(8,128)(2,1)S(1)}, u32[]{:S(2)}, u32[]{:S(2)}) collective-permute-start(bf16[4,64,192]{2,1,0:T(8,128)(2,1)} %get-tuple-element.69), channel_id=1, source_target_pairs={{0,16},{1,17},{2,18},{3,19},{4,20},{5,21},{6,22},{7,23},{8,24},{9,... | collective-permute-start | bytes 294920 | tf_op jit(solution)/shard_map/ppermute | solution.py:784
  69.0 1.2 collective-permute-start.8
  70.2 16.5 %collective-permute-done.6.rt = bf16[4,64,192]{2,1,0:T(8,128)(2,1)S(1)} collective-permute-done((bf16[4,64,192]{2,1,0:T(8,128)(2,1)}, bf16[4,64,192]{2,1,0:T(8,128)(2,1)S(1)}, u32[]{:S(2)}, u32[]{:S(2)}) %collective-permute-start.6) | collective-permute-done | bytes 98336 | tf_op jit(solution)/shard_map/ppermute | solution.py:784
  86.8 0.0 collective-permute-done.8.dr
  86.8 0.0 collective-permute-done.7.dn
  86.8 0.0 all-to-all-done.got
  86.8 1.4 %shard_map.328 = bf16[64,88,128]{2,1,0:T(8,128)(2,1)} custom-call(s32[1,1]{1,0:T(1,128)} %bitcast.is_weight, bf16[64,88,128]{2,1,0:T(8,128)(2,1)S(1)} %all-to-all-done.got), custom_call_target="tpu_custom_call" | custom-call | flops 10000000 | bytes 1000000 | tf_op jit(solution)/shard_map/pallas_call | solution.py:833
  88.2 0.0 copy-start
  88.2 0.0 copy-start.1
  88.2 0.0 copy-start.2
  88.2 0.0 copy-start.3
  88.2 9.7 %all-to-all-start.1 = ((bf16[64,88,128]{2,1,0:T(8,128)(2,1)}), bf16[64,88,128]{2,1,0:T(8,128)(2,1)S(1)}, u32[]{:S(2)}, u32[]{:S(2)}) async-start(bf16[64,88,128]{2,1,0:T(8,128)(2,1)} %shard_map.328), calls=%async_computation.1 | async-start | bytes 2883584 | tf_op jit(solution)/shard_map/all_to_all | solution.py:836
  97.9 0.0 copy-done
  97.9 0.0 copy-done.1
  97.9 0.0 copy-done.2
  98.0 0.0 copy-done.3
  98.0 1.2 shard_map.329
  99.1 20.5 %all-to-all-done.1.buf = bf16[64,88,128]{2,1,0:T(8,128)(2,1)S(1)} async-done(((bf16[64,88,128]{2,1,0:T(8,128)(2,1)}), bf16[64,88,128]{2,1,0:T(8,128)(2,1)S(1)}, u32[]{:S(2)}, u32[]{:S(2)}) %all-to-all-start.1) | async-done | bytes 1441824 | tf_op jit(solution)/shard_map/all_to_all | solution.py:836
  119.6 2.2 %collective-permute-start.9 = (bf16[64,88,128]{2,1,0:T(8,128)(2,1)S(1)}, bf16[64,88,128]{2,1,0:T(8,128)(2,1)S(1)}, u32[]{:S(2)}, u32[]{:S(2)}) collective-permute-start(bf16[64,88,128]{2,1,0:T(8,128)(2,1)S(1)} %all-to-all-done.1.buf), channel_id=1, source_target_pairs={{0,1},{1,0},{2,3},{3,2},{4,5},{5,4},{6,7},{7,6},{8,9},{9,8},{10,11... | collective-permute-start | bytes 4325384 | tf_op jit(solution)/shard_map/ppermute | solution.py:841
  121.8 1.5 %shard_map.331 = f32[2,864,144]{2,1,0:T(8,128)} custom-call(bf16[64,88,128]{2,1,0:T(8,128)(2,1)S(1)} %all-to-all-done.1.buf), custom_call_target="tpu_custom_call" | custom-call | flops 10000000 | bytes 1000000 | tf_op jit(solution)/shard_map/pallas_call | solution.py:842
  123.4 1.3 %collective-permute-done.9.oth = bf16[64,88,128]{2,1,0:T(8,128)(2,1)S(1)} collective-permute-done((bf16[64,88,128]{2,1,0:T(8,128)(2,1)S(1)}, bf16[64,88,128]{2,1,0:T(8,128)(2,1)S(1)}, u32[]{:S(2)}, u32[]{:S(2)}) %collective-permute-start.9) | collective-permute-done | bytes 1441824 | tf_op jit(solution)/shard_map/ppermute | solution.py:841
  124.7 2.1 %shard_map.330 = (f32[192,576]{1,0:T(8,128)}, f32[192,192]{1,0:T(8,128)}, f32[192,768]{1,0:T(8,128)}, f32[192,768]{1,0:T(8,128)}, f32[768,384]{1,0:T(8,128)}) custom-call(s32[1,1]{1,0:T(1,128)} %bitcast.1.refs_0_.core_ref, bf16[64,88,128]{2,1,0:T(8,128)(2,1)S(1)} %all-to-all-done.1.buf, bf16[64,88,128]{2,1,0:T(8,128)(2,1)S(1)} %collective-permute-done.9.oth), custom_call_target="tpu_custom_call" | custom-call | flops 10000000 | bytes 1000000 | tf_op jit(solution)/shard_map/pallas_call | solution.py:845
Async XLA Ops:
  3.4 20.9 %collective-permute-start = (bf16[4,240,192]{2,1,0:T(8,128)(2,1)}, bf16[4,240,192]{2,1,0:T(8,128)(2,1)S(1)}, u32[]{:S(2)}, u32[]{:S(2)}) collective-permute-start(bf16[4,240,192]{2,1,0:T(8,128)(2,1)} %get-tuple-element.48), channel_id=1, source_target_pairs={{0,15},{1,0},{2,1},{3,2},{4,3},{5,4},{6,5},{7,6},{8,7},{9,8},{10,9... | collective-permute-start | bytes 1105928 | tf_op jit(solution)/shard_map/ppermute | solution.py:784
  4.8 19.5 %collective-permute-start.1 = (bf16[272,192]{1,0:T(8,128)(2,1)}, bf16[272,192]{1,0:T(8,128)(2,1)S(1)}, u32[]{:S(2)}, u32[]{:S(2)}) collective-permute-start(bf16[272,192]{1,0:T(8,128)(2,1)} %get-tuple-element.49), channel_id=1, source_target_pairs={{0,112},{1,113},{2,114},{3,115},{4,116},{5,117},{6,118},{7,119},{8... | collective-permute-start | bytes 313352 | tf_op jit(solution)/shard_map/ppermute | solution.py:784
  10.7 13.6 %collective-permute-start.3 = (bf16[272,192]{1,0:T(8,128)(2,1)}, bf16[272,192]{1,0:T(8,128)(2,1)S(1)}, u32[]{:S(2)}, u32[]{:S(2)}) collective-permute-start(bf16[272,192]{1,0:T(8,128)(2,1)} %get-tuple-element.51), channel_id=1, source_target_pairs={{0,127},{1,112},{2,113},{3,114},{4,115},{5,116},{6,117},{7,118},{8... | collective-permute-start | bytes 313352 | tf_op jit(solution)/shard_map/ppermute | solution.py:784
  14.1 8.2 %collective-permute-start.2 = (bf16[80,192]{1,0:T(8,128)(2,1)}, bf16[80,192]{1,0:T(8,128)(2,1)S(1)}, u32[]{:S(2)}, u32[]{:S(2)}) collective-permute-start(bf16[80,192]{1,0:T(8,128)(2,1)} %get-tuple-element.50), channel_id=1, source_target_pairs={{0,16},{1,17},{2,18},{3,19},{4,20},{5,21},{6,22},{7,23},{8,24},{9,... | collective-permute-start | bytes 92168 | tf_op jit(solution)/shard_map/ppermute | solution.py:784
  17.3 7.0 %collective-permute-start.4 = (bf16[80,192]{1,0:T(8,128)(2,1)}, bf16[80,192]{1,0:T(8,128)(2,1)S(1)}, u32[]{:S(2)}, u32[]{:S(2)}) collective-permute-start(bf16[80,192]{1,0:T(8,128)(2,1)} %get-tuple-element.52), channel_id=1, source_target_pairs={{0,31},{1,16},{2,17},{3,18},{4,19},{5,20},{6,21},{7,22},{8,23},{9,... | collective-permute-start | bytes 92168 | tf_op jit(solution)/shard_map/ppermute | solution.py:784
  22.3 2.1 %copy-start.9 = (bf16[80,192]{1,0:T(8,128)(2,1)}, bf16[80,192]{1,0:T(8,128)(2,1)S(1)}, u32[]{:S(2)}) copy-start(bf16[80,192]{1,0:T(8,128)(2,1)S(1)} %collective-permute-done.2.refs_4_) | copy-start | bytes 92164
  24.3 0.6 copy-start.10
  24.3 0.7 copy-start.7
  24.3 0.7 copy-start.8
  24.3 0.8 copy-start.6
  41.5 8.3 %collective-permute-start.5 = (bf16[2560,128]{1,0:T(8,128)(2,1)}, bf16[2560,128]{1,0:T(8,128)(2,1)S(1)}, u32[]{:S(2)}, u32[]{:S(2)}) collective-permute-start(bf16[2560,128]{1,0:T(8,128)(2,1)} %get-tuple-element.59), channel_id=1, source_target_pairs={{0,1},{1,0},{2,3},{3,2},{4,5},{5,4},{6,7},{7,6},{8,9},{9,8},{10,11... | collective-permute-start | bytes 1966088 | tf_op jit(solution)/shard_map/ppermute | solution.py:820
  41.6 8.2 %copy-start.5 = (bf16[2560,128]{1,0:T(8,128)(2,1)S(1)}, bf16[2560,128]{1,0:T(8,128)(2,1)}, u32[]{:S(2)}) copy-start(bf16[2560,128]{1,0:T(8,128)(2,1)} %get-tuple-element.58) | copy-start | bytes 1966084
  49.8 1.1 copy-start.4
  52.1 34.6 %all-to-all-start = ((bf16[64,88,128]{2,1,0:T(8,128)(2,1)}), bf16[64,88,128]{2,1,0:T(8,128)(2,1)S(1)}, u32[]{:S(2)}, u32[]{:S(2)}) async-start(bf16[64,88,128]{2,1,0:T(8,128)(2,1)} %pad_maximum_fusion), calls=%async_computation | async-start | bytes 2883584 | tf_op jit(solution)/shard_map/all_to_all | solution.py:825
  64.7 22.1 %collective-permute-start.7 = (bf16[4,240,192]{2,1,0:T(8,128)(2,1)}, bf16[4,240,192]{2,1,0:T(8,128)(2,1)S(1)}, u32[]{:S(2)}, u32[]{:S(2)}) collective-permute-start(bf16[4,240,192]{2,1,0:T(8,128)(2,1)} %get-tuple-element.70), channel_id=1, source_target_pairs={{0,1},{1,2},{2,3},{3,4},{4,5},{5,6},{6,7},{7,8},{8,9},{9,10},{10,1... | collective-permute-start | bytes 1105928 | tf_op jit(solution)/shard_map/ppermute | solution.py:784
  66.6 20.2 %collective-permute-start.6 = (bf16[4,64,192]{2,1,0:T(8,128)(2,1)}, bf16[4,64,192]{2,1,0:T(8,128)(2,1)S(1)}, u32[]{:S(2)}, u32[]{:S(2)}) collective-permute-start(bf16[4,64,192]{2,1,0:T(8,128)(2,1)} %get-tuple-element.69), channel_id=1, source_target_pairs={{0,16},{1,17},{2,18},{3,19},{4,20},{5,21},{6,22},{7,23},{8,24},{9,... | collective-permute-start | bytes 294920 | tf_op jit(solution)/shard_map/ppermute | solution.py:784
  69.0 17.8 %collective-permute-start.8 = (bf16[4,64,192]{2,1,0:T(8,128)(2,1)}, bf16[4,64,192]{2,1,0:T(8,128)(2,1)S(1)}, u32[]{:S(2)}, u32[]{:S(2)}) collective-permute-start(bf16[4,64,192]{2,1,0:T(8,128)(2,1)} %get-tuple-element.71), channel_id=1, source_target_pairs={{0,17},{1,18},{2,19},{3,20},{4,21},{5,22},{6,23},{7,24},{8,25},{9,... | collective-permute-start | bytes 294920 | tf_op jit(solution)/shard_map/ppermute | solution.py:784
  88.2 9.7 %copy-start = (bf16[288,512]{1,0:T(8,128)(2,1)S(1)}, bf16[288,512]{1,0:T(8,128)(2,1)}, u32[]{:S(2)}) copy-start(bf16[288,512]{1,0:T(8,128)(2,1)} %constant.70.clone.m_pm) | copy-start | bytes 884740
  88.2 9.8 %copy-start.1 = (bf16[4,144,192]{2,1,0:T(8,128)(2,1)S(1)}, bf16[4,144,192]{2,1,0:T(8,128)(2,1)}, u32[]{:S(2)}) copy-start(bf16[4,144,192]{2,1,0:T(8,128)(2,1)} %get-tuple-element.73.keep_t) | copy-start | bytes 663556
  88.2 9.8 %copy-start.2 = (bf16[4,48,384]{2,1,0:T(8,128)(2,1)S(1)}, bf16[4,48,384]{2,1,0:T(8,128)(2,1)}, u32[]{:S(2)}) copy-start(bf16[4,48,384]{2,1,0:T(8,128)(2,1)} %get-tuple-element.74.keep_m) | copy-start | bytes 442372
  88.2 9.8 %copy-start.3 = (bf16[144,32]{1,0:T(8,128)(2,1)S(1)}, bf16[144,32]{1,0:T(8,128)(2,1)}, u32[]{:S(2)}) copy-start(bf16[144,32]{1,0:T(8,128)(2,1)} %constant.69.clone.m_place) | copy-start | bytes 27652
  88.2 31.4 %all-to-all-start.1 = ((bf16[64,88,128]{2,1,0:T(8,128)(2,1)}), bf16[64,88,128]{2,1,0:T(8,128)(2,1)S(1)}, u32[]{:S(2)}, u32[]{:S(2)}) async-start(bf16[64,88,128]{2,1,0:T(8,128)(2,1)} %shard_map.328), calls=%async_computation.1 | async-start | bytes 2883584 | tf_op jit(solution)/shard_map/all_to_all | solution.py:836
  119.6 5.1 %collective-permute-start.9 = (bf16[64,88,128]{2,1,0:T(8,128)(2,1)S(1)}, bf16[64,88,128]{2,1,0:T(8,128)(2,1)S(1)}, u32[]{:S(2)}, u32[]{:S(2)}) collective-permute-start(bf16[64,88,128]{2,1,0:T(8,128)(2,1)S(1)} %all-to-all-done.1.buf), channel_id=1, source_target_pairs={{0,1},{1,0},{2,3},{3,2},{4,5},{5,4},{6,7},{7,6},{8,9},{9,8},{10,11... | collective-permute-start | bytes 4325384 | tf_op jit(solution)/shard_map/ppermute | solution.py:841

commit v2 on v1

--- a/solution.py
+++ b/solution.py
@@ -507,19 +507,22 @@
     xs = xn[...].reshape(8 * WT, D)
     parts = [tn(xs, dqkv[part].reshape(8 * WT, D)) for part in range(3)]
     value = jnp.concatenate(parts, axis=1).astype(BF16)
+    def put(start, block):
+        for n in range(block.shape[0] // SECOND):
+            grads[start // SECOND + n, 0:SECOND] = block[n * SECOND : n * SECOND + SECOND]
+
     for t in range(4):
-        grads[t * D : t * D + D] = value[:, t * 128 : t * 128 + 128]
-    grads[768:960, 0:64] = value[:, 512:576]
-    grads[768:960, 64:128] = jnp.zeros((D, 64), BF16)
+        put(t * D, value[:, t * 128 : t * 128 + 128])
+    put(768, jnp.concatenate([value[:, 512:576], jnp.zeros((D, 64), BF16)], axis=1))
     for z in range(2):
         total = gb[z].astype(BF16)
         for t in range(7):
             tile = total[:, t * 128 : min(t * 128 + 128, HQ)]
             if t == 6:
                 tile = jnp.concatenate([tile, jnp.zeros((WT, 896 - HQ), BF16)], axis=1)
-            at = BIAS_AT + (z * 7 + t) * WT
-            grads[at : at + WT] = tile
-    grads[BIAS_AT + 14 * WT :] = jnp.zeros((PEERS * SECOND - BIAS_AT - 14 * WT, 128), BF16)
+            put(BIAS_AT + (z * 7 + t) * WT, tile)
+    end = BIAS_AT + 14 * WT
+    put(end, jnp.zeros((PEERS * SECOND - end, 128), BF16))
 
 
 def third_kernel(
@@ -571,24 +574,24 @@
 
 def add_kernel(is_weight, got, out, *, bands):
     count = got.shape[0]
-    mine = got[0, 0:FIRST].astype(F32)
+    mine = got[0, SECOND:ROWS].astype(F32)
     for n in range(1, count):
-        mine = mine + got[n, 0:FIRST].astype(F32)
+        mine = mine + got[n, SECOND:ROWS].astype(F32)
     mine = mine.astype(BF16)
     total = 0.0
     parts = []
     for b in range(bands):
-        part = got[b, FIRST:ROWS].astype(F32)
+        part = got[b, 0:SECOND].astype(F32)
         for n in range(b + bands, count, bands):
-            part = part + got[n, FIRST:ROWS].astype(F32)
+            part = part + got[n, 0:SECOND].astype(F32)
         parts.append(part)
         total = total + part
     flag = is_weight[0, 0] > 0
     for b in range(bands):
         part = jnp.where(flag, total, parts[b]).astype(BF16)
         for n in range(b, count, bands):
-            out[n, 0:FIRST] = mine
-            out[n, FIRST:ROWS] = part
+            out[n, SECOND:ROWS] = mine
+            out[n, 0:SECOND] = part
 
 
 def pieces(start, count, size):
@@ -601,7 +604,7 @@
 
 def bias_kernel(buf, gbias, *, scale):
     def rows(start, count):
-        got = [buf[c, FIRST + off : FIRST + off + n].astype(F32) for c, off, n in pieces(start, count, SECOND)]
+        got = [buf[c, off : off + n].astype(F32) for c, off, n in pieces(start, count, SECOND)]
         return jnp.concatenate(got, axis=0)
 
     for z in range(2):
@@ -617,14 +620,14 @@
     def first(half, start, count):
         got = []
         for c, off, n in pieces(start, count, FIRST):
-            got.append(jnp.where(here == half, buf[c, off : off + n], oth[c, off : off + n]).astype(F32))
+            at = SECOND + off
+            got.append(jnp.where(here == half, buf[c, at : at + n], oth[c, at : at + n]).astype(F32))
         return jnp.concatenate(got, axis=0) * scale
 
     def second(start, count):
         got = []
         for c, off, n in pieces(start, count, SECOND):
-            at = FIRST + off
-            got.append(buf[c, at : at + n].astype(F32) + oth[c, at : at + n].astype(F32))
+            got.append(buf[c, off : off + n].astype(F32) + oth[c, off : off + n].astype(F32))
         return jnp.concatenate(got, axis=0) * scale
 
     for t in range(6):
@@ -742,7 +745,7 @@
     count = len(operands)
     return call(
         staged(second_kernel, count),
-        (shape(PEERS * SECOND, 128), shape(3, 8, WT, D)),
+        (shape(PEERS, ROWS, 128), shape(3, 8, WT, D)),
         [
             pltpu.VMEM((2, WT, HQ), F32),
         ]
@@ -818,16 +821,16 @@
         quad_map(), cot, cot_map(), gain_two.reshape(1, D), w_fc1, w_fc2.T, gain_merge.reshape(1, FF), w_merge, back_map(),
     )
     arrived = lax.ppermute(leave, "core", [(0, 1), (1, 0)])
-    second, dqkv = second_call()(w3, wt3, w_proj, xn, datt, head, prob)
-    arrived, second = lax.optimization_barrier((arrived, second))
+    grads, dqkv = second_call()(w3, wt3, w_proj, xn, datt, head, prob)
+    arrived, grads = lax.optimization_barrier((arrived, grads))
     first = (first.astype(F32) + arrived.astype(F32)).astype(BF16).reshape(PEERS, FIRST, 128)
-    grads = jnp.concatenate([first, second.reshape(PEERS, SECOND, 128)], axis=1)
+    grads = lax.dynamic_update_slice(grads, first, (0, SECOND, 0))
     grads = lax.all_to_all(grads, peers, 0, 0)
     keep_t, keep_m, rt, dn, dr = third_call()(tok8, datt, dqkv, merged, g1, w_qkv, out_map(), merged_map())
     rt = move(rt, 1, 0)
     dn = move(dn, 0, 1)
     dr = move(dr, 1, 1)
-    grads, rt, dn, dr = lax.optimization_barrier((grads, rt, dn, dr))
+    grads, keep_t = lax.optimization_barrier((grads, keep_t))
     place = lax.axis_index(peers)
     is_weight = (place < BIAS_AT // SECOND).astype(jnp.int32).reshape(1, 1)
     grads = call(

time: 127 us -> 122 us (0.961)
  starting transfers between devices: 39 us -> 34.3 us
    ppermute x8, waiting for transfers between devices: 18.6 us -> 23.1 us  [move(): return lax.ppermute(block, ('lon',) + LAT, route)]
    all_to_all x2, starting transfers between devices: 17.1 us -> 12.8 us  [body(): grads = lax.all_to_all(grads, peers, 0, 0)]
    all_to_all x2, waiting for transfers between devices: 20.5 us -> 16.6 us  [body(): grads = lax.all_to_all(grads, peers, 0, 0)]
    ppermute x1, starting transfers between devices: 2.23 us -> 0.94 us  [body(): other = lax.ppermute(grads, 'core', [(0, 1), (1, 0)])]
  transfers between devices with their start and end apart: 12 -> 12, of which waited for: 4 -> 5; matrix products, arithmetic and copies ran while one was open for 1% -> 1% of each run, Pallas kernels for 16% -> 16%
where the time goes in v2:
time: 122 us
  Pallas kernels  42.5 us (35%)
  waiting for transfers between devices  41 us (34%)
  starting transfers between devices  34.3 us (28%)
  local copies, waits for them, and re-layouts  3.18 us (3%)
    ppermute x8, waiting for transfers between devices, move(): return lax.ppermute(block, ('lon',) + LAT, route)  23.1 us
    ppermute x8, starting transfers between devices, move(): return lax.ppermute(block, ('lon',) + LAT, route)  20.5 us
    all_to_all x2, waiting for transfers between devices, body(): grads = lax.all_to_all(grads, peers, 0, 0)  16.6 us
    pallas_call x1, Pallas kernels, body(): first_call()  16.3 us
    all_to_all x2, starting transfers between devices, body(): grads = lax.all_to_all(grads, peers, 0, 0)  12.8 us
    pallas_call x1, Pallas kernels, body(): grads, dqkv = second_call()(w3, wt3, w_proj, xn, datt, head, prob)  8.42 us
    pallas_call x1, Pallas kernels, body(): third_call()(tok8, datt, dqkv, merged, g1, w_qkv, out_map(), merged_map())  5.13 us
    pallas_call x1, Pallas kernels, body(): call(prepare_kernel, (shape(3, D, D), shape(3, D, D), shape(2, WT, HQ, ki...  3.67 us
  transfers between devices with their start and end apart: 12, of which 5 were waited for; matrix products, arithmetic and copies ran while one was open for 1% of the time, Pallas kernels for 16%

profile of v2, /device:TPU:1, one launch (start us, length us, event | category | flops | bytes accessed | tf_op | source)
XLA Modules:
  0.0 121.9 jit_solution(5869769348740476854)
XLA Ops:
  0.6 2.7 %shard_map.323 = (bf16[4,240,192]{2,1,0:T(8,128)(2,1)}, bf16[272,192]{1,0:T(8,128)(2,1)}, bf16[80,192]{1,0:T(8,128)(2,1)}, bf16[272,192]{1,0:T(8,128)(2,1)}, bf1...) custom-call(bf16[4,288,192]{2,1,0:T(8,128)(2,1)} %bitcast.21, bf16[72,4,384]{2,1,0:T(4,128)(2,1)} %bitcast.23, ...), custom_call_target="tpu_custom_call" | custom-call | flops 10000000 | bytes 1000000 | tf_op jit(solution)/shard_map/pallas_call | solution.py:789
  3.4 1.4 %collective-permute-start = (bf16[4,240,192]{2,1,0:T(8,128)(2,1)}, bf16[4,240,192]{2,1,0:T(8,128)(2,1)S(1)}, u32[]{:S(2)}, u32[]{:S(2)}) collective-permute-start(bf16[4,240,192]{2,1,0:T(8,128)(2,1)} %get-tuple-element.46), channel_id=1, source_target_pairs={{0,15},{1,0},{2,1},{3,2},{4,3},{5,4},{6,5},{7,6},{8,7},{9,8},{10,9... | collective-permute-start | bytes 1105928 | tf_op jit(solution)/shard_map/ppermute | solution.py:787
  4.8 5.9 %collective-permute-start.1 = (bf16[272,192]{1,0:T(8,128)(2,1)}, bf16[272,192]{1,0:T(8,128)(2,1)S(1)}, u32[]{:S(2)}, u32[]{:S(2)}) collective-permute-start(bf16[272,192]{1,0:T(8,128)(2,1)} %get-tuple-element.47), channel_id=1, source_target_pairs={{0,112},{1,113},{2,114},{3,115},{4,116},{5,117},{6,118},{7,119},{8... | collective-permute-start | bytes 313352 | tf_op jit(solution)/shard_map/ppermute | solution.py:787
  10.7 3.4 %collective-permute-start.3 = (bf16[272,192]{1,0:T(8,128)(2,1)}, bf16[272,192]{1,0:T(8,128)(2,1)S(1)}, u32[]{:S(2)}, u32[]{:S(2)}) collective-permute-start(bf16[272,192]{1,0:T(8,128)(2,1)} %get-tuple-element.49), channel_id=1, source_target_pairs={{0,127},{1,112},{2,113},{3,114},{4,115},{5,116},{6,117},{7,118},{8... | collective-permute-start | bytes 313352 | tf_op jit(solution)/shard_map/ppermute | solution.py:787
  14.1 3.2 %collective-permute-start.2 = (bf16[80,192]{1,0:T(8,128)(2,1)}, bf16[80,192]{1,0:T(8,128)(2,1)S(1)}, u32[]{:S(2)}, u32[]{:S(2)}) collective-permute-start(bf16[80,192]{1,0:T(8,128)(2,1)} %get-tuple-element.48), channel_id=1, source_target_pairs={{0,16},{1,17},{2,18},{3,19},{4,20},{5,21},{6,22},{7,23},{8,24},{9,... | collective-permute-start | bytes 92168 | tf_op jit(solution)/shard_map/ppermute | solution.py:787
  17.3 0.0 collective-permute-start.4
  17.3 1.3 %reshape.69.refs_26_ = f32[1,768]{1,0:T(1,128)} reshape(f32[768]{0:T(1024)} %param.36) | data formatting | bytes 6144 | tf_op jit(solution)/shard_map/reshape | solution.py:821
  18.6 3.7 %shard_map.324 = (bf16[3,192,192]{2,1,0:T(8,128)(2,1)}, bf16[3,192,192]{2,1,0:T(8,128)(2,1)}, f32[2,144,864]{2,1,0:T(8,128)}, f32[2,2,144,144]{3,2,1,0:T(8,128)}) custom-call(s32[1,1]{1,0:T(1,128)} %bitcast.6.bottom_ref, bf16[192,576]{1,0:T(8,128)(2,1)} %wqkv.3, f32[2,864,144]{2,1,0:T(8,128)} %bitcast.20), custom_call_target="tpu_custom_call" | custom-call | flops 10000000 | bytes 1000000 | tf_op jit(solution)/shard_map/pallas_call | solution.py:810
  22.3 0.0 collective-permute-done.2.refs_4_
  22.3 0.0 copy-start.11
  22.3 2.0 %collective-permute-done.4.refs_6_ = bf16[80,192]{1,0:T(8,128)(2,1)S(1)} collective-permute-done((bf16[80,192]{1,0:T(8,128)(2,1)}, bf16[80,192]{1,0:T(8,128)(2,1)S(1)}, u32[]{:S(2)}, u32[]{:S(2)}) %collective-permute-start.4) | collective-permute-done | bytes 30752 | tf_op jit(solution)/shard_map/ppermute | solution.py:787
  24.3 0.0 copy-start.12
  24.3 0.0 collective-permute-done.1.refs_3_
  24.3 0.0 copy-start.7
  24.3 0.0 collective-permute-done.3.refs_5_
  24.3 0.0 copy-start.8
  24.3 0.0 collective-permute-done.refs_2_
  24.3 0.0 copy-start.5
  24.3 0.0 copy-done.11
  24.3 0.6 copy-done.12
  24.9 0.1 copy-done.7
  24.9 0.0 copy-done.8
  25.0 0.2 copy-done.5
  25.2 16.3 %shard_map.325 = (bf16[2560,128]{1,0:T(8,128)(2,1)}, bf16[2560,128]{1,0:T(8,128)(2,1)}, bf16[320,384]{1,0:T(8,128)(2,1)}, bf16[8,144,192]{2,1,0:T(8,128)(2,1)}, ...) custom-call(s32[1,1]{1,0:T(1,128)} %bitcast.1.refs_0_.core_ref, ...), custom_call_target="tpu_custom_call" | custom-call | flops 20000000000 | bytes 10000000 | tf_op jit(solution)/shard_map/pallas_call | solution.py:817
  41.5 0.1 collective-permute-start.5
  41.6 0.0 copy-start.4
  41.6 8.4 %shard_map.326 = (bf16[64,88,128]{2,1,0:T(8,128)(2,1)}, bf16[3,8,144,192]{3,2,1,0:T(8,128)(2,1)}) custom-call(bf16[3,192,192]{2,1,0:T(8,128)(2,1)} %get-tuple-element.51.refs_9_.refs_0_, bf16[3,192,192]{2,1,0:T(8,128)(2,1)} %get-tuple-element.52.refs_10_.refs_1_, bf16[192,192]{1,0:T(8,128)(2,1)} %refs_2_.1, bf16[8,144,192]{2,1,0:T(8,128)(2,1)} %get-tuple-element.57.refs_3_, ...), custom_call_target="tpu_custom_call" | custom-call | flops 10000000000 | bytes 10000000 | tf_op jit(solution)/shard_map/pallas_call | solution.py:824
  50.0 0.0 collective-permute-done.5
  50.0 0.0 copy-done.4
  50.0 0.2 add_convert_fusion
  50.2 1.0 constant_dynamic-update-slice_fusion
  51.2 7.4 %all-to-all-start = ((bf16[64,88,128]{2,1,0:T(8,128)(2,1)}), bf16[64,88,128]{2,1,0:T(8,128)(2,1)S(1)}, u32[]{:S(2)}, u32[]{:S(2)}) async-start(bf16[64,88,128]{2,1,0:T(8,128)(2,1)} %constant_dynamic-update-slice_fusion), calls=%async_computation | async-start | bytes 2883584 | tf_op jit(solution)/shard_map/all_to_all | solution.py:828
  58.6 5.1 %shard_map.327 = (bf16[4,144,192]{2,1,0:T(8,128)(2,1)}, bf16[4,48,384]{2,1,0:T(8,128)(2,1)}, bf16[4,64,192]{2,1,0:T(8,128)(2,1)}, bf16[4,240,192]{2,1,0:T(8,128)(2,1)}, bf16[4,64,192]{2,1,0:T(8,128)(2,1)}) custom-call(bf16[8,144,192]{2,1,0:T(8,128)(2,1)} %get-tuple-element.64.tok8, bf16[8,144,192]{2,1,0:T(8,128)(2,1)} %get-tuple-element.58.refs_4_.datt, ...), custom_call_target="tpu_custom_call" | custom-call | flops 10000000000 | bytes 10000000 | tf_op jit(solution)/shard_map/pallas_call | solution.py:829
  63.8 16.6 %all-to-all-done.got = bf16[64,88,128]{2,1,0:T(8,128)(2,1)S(1)} async-done(((bf16[64,88,128]{2,1,0:T(8,128)(2,1)}), bf16[64,88,128]{2,1,0:T(8,128)(2,1)S(1)}, u32[]{:S(2)}, u32[]{:S(2)}) %all-to-all-start) | async-done | bytes 1441824 | tf_op jit(solution)/shard_map/all_to_all | solution.py:828
  80.4 1.4 %shard_map.328 = bf16[64,88,128]{2,1,0:T(8,128)(2,1)} custom-call(s32[1,1]{1,0:T(1,128)} %bitcast.is_weight, bf16[64,88,128]{2,1,0:T(8,128)(2,1)S(1)} %all-to-all-done.got), custom_call_target="tpu_custom_call" | custom-call | flops 10000000 | bytes 1000000 | tf_op jit(solution)/shard_map/pallas_call | solution.py:836
  81.8 0.0 copy-start.6
  81.8 0.0 copy-start.10
  81.8 0.0 copy-start.9
  81.8 0.0 copy-start
  81.8 0.0 copy-start.1
  81.8 0.0 copy-start.2
  81.8 0.0 copy-start.3
  81.8 5.4 %all-to-all-start.1 = ((bf16[64,88,128]{2,1,0:T(8,128)(2,1)}), bf16[64,88,128]{2,1,0:T(8,128)(2,1)S(1)}, u32[]{:S(2)}, u32[]{:S(2)}) async-start(bf16[64,88,128]{2,1,0:T(8,128)(2,1)} %shard_map.328), calls=%async_computation.1 | async-start | bytes 2883584 | tf_op jit(solution)/shard_map/all_to_all | solution.py:839
  87.2 0.0 copy-done.6
  87.2 2.8 %collective-permute-start.7 = (bf16[4,240,192]{2,1,0:T(8,128)(2,1)S(1)}, bf16[4,240,192]{2,1,0:T(8,128)(2,1)S(1)}, u32[]{:S(2)}, u32[]{:S(2)}) collective-permute-start(bf16[4,240,192]{2,1,0:T(8,128)(2,1)S(1)} %copy-done.6), channel_id=1, source_target_pairs={{0,1},{1,2},{2,3},{3,4},{4,5},{5,6},{6,7},{7,8},{8,9},{9,10},{10,1... | collective-permute-start | bytes 1105928 | tf_op jit(solution)/shard_map/ppermute | solution.py:787
  90.0 0.0 copy-done.10
  90.0 2.4 %collective-permute-start.6 = (bf16[4,64,192]{2,1,0:T(8,128)(2,1)S(1)}, bf16[4,64,192]{2,1,0:T(8,128)(2,1)S(1)}, u32[]{:S(2)}, u32[]{:S(2)}) collective-permute-start(bf16[4,64,192]{2,1,0:T(8,128)(2,1)S(1)} %copy-done.10), channel_id=1, source_target_pairs={{0,16},{1,17},{2,18},{3,19},{4,20},{5,21},{6,22},{7,23},{8,24},{9,... | collective-permute-start | bytes 294920 | tf_op jit(solution)/shard_map/ppermute | solution.py:787
  92.4 0.0 copy-done.9
  92.4 1.3 %collective-permute-start.8 = (bf16[4,64,192]{2,1,0:T(8,128)(2,1)S(1)}, bf16[4,64,192]{2,1,0:T(8,128)(2,1)S(1)}, u32[]{:S(2)}, u32[]{:S(2)}) collective-permute-start(bf16[4,64,192]{2,1,0:T(8,128)(2,1)S(1)} %copy-done.9), channel_id=1, source_target_pairs={{0,17},{1,18},{2,19},{3,20},{4,21},{5,22},{6,23},{7,24},{8,25},{9,... | collective-permute-start | bytes 294920 | tf_op jit(solution)/shard_map/ppermute | solution.py:787
  93.7 20.4 %collective-permute-done.6.rt = bf16[4,64,192]{2,1,0:T(8,128)(2,1)S(1)} collective-permute-done((bf16[4,64,192]{2,1,0:T(8,128)(2,1)S(1)}, bf16[4,64,192]{2,1,0:T(8,128)(2,1)S(1)}, u32[]{:S(2)}, u32[]{:S(2)}) %collective-permute-start.6) | collective-permute-done | bytes 98336 | tf_op jit(solution)/shard_map/ppermute | solution.py:787
  114.1 0.7 collective-permute-done.8.dr
  114.8 0.0 collective-permute-done.7.dn
  114.8 0.0 copy-done
  114.8 0.0 copy-done.1
  114.8 0.0 copy-done.2
  114.9 0.0 copy-done.3
  114.9 1.2 shard_map.329
  116.1 0.0 all-to-all-done.1.buf
  116.1 0.9 collective-permute-start.9
  117.0 1.5 %shard_map.331 = f32[2,864,144]{2,1,0:T(8,128)} custom-call(bf16[64,88,128]{2,1,0:T(8,128)(2,1)S(1)} %all-to-all-done.1.buf), custom_call_target="tpu_custom_call" | custom-call | flops 10000000 | bytes 1000000 | tf_op jit(solution)/shard_map/pallas_call | solution.py:845
  118.5 1.3 %collective-permute-done.9.oth = bf16[64,88,128]{2,1,0:T(8,128)(2,1)S(1)} collective-permute-done((bf16[64,88,128]{2,1,0:T(8,128)(2,1)S(1)}, bf16[64,88,128]{2,1,0:T(8,128)(2,1)S(1)}, u32[]{:S(2)}, u32[]{:S(2)}) %collective-permute-start.9) | collective-permute-done | bytes 1441824 | tf_op jit(solution)/shard_map/ppermute | solution.py:844
  119.8 2.1 %shard_map.330 = (f32[192,576]{1,0:T(8,128)}, f32[192,192]{1,0:T(8,128)}, f32[192,768]{1,0:T(8,128)}, f32[192,768]{1,0:T(8,128)}, f32[768,384]{1,0:T(8,128)}) custom-call(s32[1,1]{1,0:T(1,128)} %bitcast.1.refs_0_.core_ref, bf16[64,88,128]{2,1,0:T(8,128)(2,1)S(1)} %all-to-all-done.1.buf, bf16[64,88,128]{2,1,0:T(8,128)(2,1)S(1)} %collective-permute-done.9.oth), custom_call_target="tpu_custom_call" | custom-call | flops 10000000 | bytes 1000000 | tf_op jit(solution)/shard_map/pallas_call | solution.py:848
Async XLA Ops:
  3.4 20.9 %collective-permute-start = (bf16[4,240,192]{2,1,0:T(8,128)(2,1)}, bf16[4,240,192]{2,1,0:T(8,128)(2,1)S(1)}, u32[]{:S(2)}, u32[]{:S(2)}) collective-permute-start(bf16[4,240,192]{2,1,0:T(8,128)(2,1)} %get-tuple-element.46), channel_id=1, source_target_pairs={{0,15},{1,0},{2,1},{3,2},{4,3},{5,4},{6,5},{7,6},{8,7},{9,8},{10,9... | collective-permute-start | bytes 1105928 | tf_op jit(solution)/shard_map/ppermute | solution.py:787
  4.8 19.5 %collective-permute-start.1 = (bf16[272,192]{1,0:T(8,128)(2,1)}, bf16[272,192]{1,0:T(8,128)(2,1)S(1)}, u32[]{:S(2)}, u32[]{:S(2)}) collective-permute-start(bf16[272,192]{1,0:T(8,128)(2,1)} %get-tuple-element.47), channel_id=1, source_target_pairs={{0,112},{1,113},{2,114},{3,115},{4,116},{5,117},{6,118},{7,119},{8... | collective-permute-start | bytes 313352 | tf_op jit(solution)/shard_map/ppermute | solution.py:787
  10.7 13.6 %collective-permute-start.3 = (bf16[272,192]{1,0:T(8,128)(2,1)}, bf16[272,192]{1,0:T(8,128)(2,1)S(1)}, u32[]{:S(2)}, u32[]{:S(2)}) collective-permute-start(bf16[272,192]{1,0:T(8,128)(2,1)} %get-tuple-element.49), channel_id=1, source_target_pairs={{0,127},{1,112},{2,113},{3,114},{4,115},{5,116},{6,117},{7,118},{8... | collective-permute-start | bytes 313352 | tf_op jit(solution)/shard_map/ppermute | solution.py:787
  14.1 8.2 %collective-permute-start.2 = (bf16[80,192]{1,0:T(8,128)(2,1)}, bf16[80,192]{1,0:T(8,128)(2,1)S(1)}, u32[]{:S(2)}, u32[]{:S(2)}) collective-permute-start(bf16[80,192]{1,0:T(8,128)(2,1)} %get-tuple-element.48), channel_id=1, source_target_pairs={{0,16},{1,17},{2,18},{3,19},{4,20},{5,21},{6,22},{7,23},{8,24},{9,... | collective-permute-start | bytes 92168 | tf_op jit(solution)/shard_map/ppermute | solution.py:787
  17.3 7.0 %collective-permute-start.4 = (bf16[80,192]{1,0:T(8,128)(2,1)}, bf16[80,192]{1,0:T(8,128)(2,1)S(1)}, u32[]{:S(2)}, u32[]{:S(2)}) collective-permute-start(bf16[80,192]{1,0:T(8,128)(2,1)} %get-tuple-element.50), channel_id=1, source_target_pairs={{0,31},{1,16},{2,17},{3,18},{4,19},{5,20},{6,21},{7,22},{8,23},{9,... | collective-permute-start | bytes 92168 | tf_op jit(solution)/shard_map/ppermute | solution.py:787
  22.3 2.1 %copy-start.11 = (bf16[80,192]{1,0:T(8,128)(2,1)}, bf16[80,192]{1,0:T(8,128)(2,1)S(1)}, u32[]{:S(2)}) copy-start(bf16[80,192]{1,0:T(8,128)(2,1)S(1)} %collective-permute-done.2.refs_4_) | copy-start | bytes 92164
  24.3 0.6 copy-start.12
  24.3 0.7 copy-start.7
  24.3 0.7 copy-start.8
  24.3 0.8 copy-start.5
  41.5 8.5 %collective-permute-start.5 = (bf16[2560,128]{1,0:T(8,128)(2,1)}, bf16[2560,128]{1,0:T(8,128)(2,1)S(1)}, u32[]{:S(2)}, u32[]{:S(2)}) collective-permute-start(bf16[2560,128]{1,0:T(8,128)(2,1)} %get-tuple-element.56), channel_id=1, source_target_pairs={{0,1},{1,0},{2,3},{3,2},{4,5},{5,4},{6,7},{7,6},{8,9},{9,8},{10,11... | collective-permute-start | bytes 1966088 | tf_op jit(solution)/shard_map/ppermute | solution.py:823
  41.6 8.5 %copy-start.4 = (bf16[2560,128]{1,0:T(8,128)(2,1)S(1)}, bf16[2560,128]{1,0:T(8,128)(2,1)}, u32[]{:S(2)}) copy-start(bf16[2560,128]{1,0:T(8,128)(2,1)} %get-tuple-element.62) | copy-start | bytes 1966084
  51.2 29.1 %all-to-all-start = ((bf16[64,88,128]{2,1,0:T(8,128)(2,1)}), bf16[64,88,128]{2,1,0:T(8,128)(2,1)S(1)}, u32[]{:S(2)}, u32[]{:S(2)}) async-start(bf16[64,88,128]{2,1,0:T(8,128)(2,1)} %constant_dynamic-update-slice_fusion), calls=%async_computation | async-start | bytes 2883584 | tf_op jit(solution)/shard_map/all_to_all | solution.py:828
  81.8 5.4 %copy-start.6 = (bf16[4,240,192]{2,1,0:T(8,128)(2,1)S(1)}, bf16[4,240,192]{2,1,0:T(8,128)(2,1)}, u32[]{:S(2)}) copy-start(bf16[4,240,192]{2,1,0:T(8,128)(2,1)} %get-tuple-element.72) | copy-start | bytes 1105924
  81.8 8.2 %copy-start.10 = (bf16[4,64,192]{2,1,0:T(8,128)(2,1)S(1)}, bf16[4,64,192]{2,1,0:T(8,128)(2,1)}, u32[]{:S(2)}) copy-start(bf16[4,64,192]{2,1,0:T(8,128)(2,1)} %get-tuple-element.71) | copy-start | bytes 294916
  81.8 10.6 %copy-start.9 = (bf16[4,64,192]{2,1,0:T(8,128)(2,1)S(1)}, bf16[4,64,192]{2,1,0:T(8,128)(2,1)}, u32[]{:S(2)}) copy-start(bf16[4,64,192]{2,1,0:T(8,128)(2,1)} %get-tuple-element.73) | copy-start | bytes 294916
  81.8 33.1 %copy-start = (bf16[288,512]{1,0:T(8,128)(2,1)S(1)}, bf16[288,512]{1,0:T(8,128)(2,1)}, u32[]{:S(2)}) copy-start(bf16[288,512]{1,0:T(8,128)(2,1)} %constant.74.clone.m_pm) | copy-start | bytes 884740
  81.8 33.1 %copy-start.1 = (bf16[4,144,192]{2,1,0:T(8,128)(2,1)S(1)}, bf16[4,144,192]{2,1,0:T(8,128)(2,1)}, u32[]{:S(2)}) copy-start(bf16[4,144,192]{2,1,0:T(8,128)(2,1)} %get-tuple-element.69.keep_t) | copy-start | bytes 663556
  81.8 33.1 %copy-start.2 = (bf16[4,48,384]{2,1,0:T(8,128)(2,1)S(1)}, bf16[4,48,384]{2,1,0:T(8,128)(2,1)}, u32[]{:S(2)}) copy-start(bf16[4,48,384]{2,1,0:T(8,128)(2,1)} %get-tuple-element.70.keep_m) | copy-start | bytes 442372
  81.8 33.1 %copy-start.3 = (bf16[144,32]{1,0:T(8,128)(2,1)S(1)}, bf16[144,32]{1,0:T(8,128)(2,1)}, u32[]{:S(2)}) copy-start(bf16[144,32]{1,0:T(8,128)(2,1)} %constant.73.clone.m_place) | copy-start | bytes 27652
  81.8 34.2 %all-to-all-start.1 = ((bf16[64,88,128]{2,1,0:T(8,128)(2,1)}), bf16[64,88,128]{2,1,0:T(8,128)(2,1)S(1)}, u32[]{:S(2)}, u32[]{:S(2)}) async-start(bf16[64,88,128]{2,1,0:T(8,128)(2,1)} %shard_map.328), calls=%async_computation.1 | async-start | bytes 2883584 | tf_op jit(solution)/shard_map/all_to_all | solution.py:839
  87.2 27.6 %collective-permute-start.7 = (bf16[4,240,192]{2,1,0:T(8,128)(2,1)S(1)}, bf16[4,240,192]{2,1,0:T(8,128)(2,1)S(1)}, u32[]{:S(2)}, u32[]{:S(2)}) collective-permute-start(bf16[4,240,192]{2,1,0:T(8,128)(2,1)S(1)} %copy-done.6), channel_id=1, source_target_pairs={{0,1},{1,2},{2,3},{3,4},{4,5},{5,6},{6,7},{7,8},{8,9},{9,10},{10,1... | collective-permute-start | bytes 1105928 | tf_op jit(solution)/shard_map/ppermute | solution.py:787
  90.0 24.2 %collective-permute-start.6 = (bf16[4,64,192]{2,1,0:T(8,128)(2,1)S(1)}, bf16[4,64,192]{2,1,0:T(8,128)(2,1)S(1)}, u32[]{:S(2)}, u32[]{:S(2)}) collective-permute-start(bf16[4,64,192]{2,1,0:T(8,128)(2,1)S(1)} %copy-done.10), channel_id=1, source_target_pairs={{0,16},{1,17},{2,18},{3,19},{4,20},{5,21},{6,22},{7,23},{8,24},{9,... | collective-permute-start | bytes 294920 | tf_op jit(solution)/shard_map/ppermute | solution.py:787
  92.4 22.4 %collective-permute-start.8 = (bf16[4,64,192]{2,1,0:T(8,128)(2,1)S(1)}, bf16[4,64,192]{2,1,0:T(8,128)(2,1)S(1)}, u32[]{:S(2)}, u32[]{:S(2)}) collective-permute-start(bf16[4,64,192]{2,1,0:T(8,128)(2,1)S(1)} %copy-done.9), channel_id=1, source_target_pairs={{0,17},{1,18},{2,19},{3,20},{4,21},{5,22},{6,23},{7,24},{8,25},{9,... | collective-permute-start | bytes 294920 | tf_op jit(solution)/shard_map/ppermute | solution.py:787
  116.1 3.8 %collective-permute-start.9 = (bf16[64,88,128]{2,1,0:T(8,128)(2,1)S(1)}, bf16[64,88,128]{2,1,0:T(8,128)(2,1)S(1)}, u32[]{:S(2)}, u32[]{:S(2)}) collective-permute-start(bf16[64,88,128]{2,1,0:T(8,128)(2,1)S(1)} %all-to-all-done.1.buf), channel_id=1, source_target_pairs={{0,1},{1,0},{2,3},{3,2},{4,5},{5,4},{6,7},{7,6},{8,9},{9,8},{10,11... | collective-permute-start | bytes 4325384 | tf_op jit(solution)/shard_map/ppermute | solution.py:844

commit v3 on v2

--- a/solution.py
+++ b/solution.py
@@ -837,10 +837,10 @@
         functools.partial(add_kernel, bands=lax.axis_size("chip")), shape(PEERS, ROWS, 128), in_specs=[SCALAR, WHOLE]
     )(is_weight, grads)
     grads = lax.all_to_all(grads, peers, 0, 0)
+    grads, rt, dn, dr = lax.optimization_barrier((grads, rt, dn, dr))
     grad_tokens, merged = call(place_kernel, (shape(4, 288, D), shape(72, 4, MG)))(
         keep_t, keep_m, rt, dn, dr, place_map(), place_merged_map()
     )
-    grads, grad_tokens, merged = lax.optimization_barrier((grads, grad_tokens, merged))
     other = lax.ppermute(grads, "core", [(0, 1), (1, 0)])
     gbias = call(
         functools.partial(bias_kernel, scale=WT * (4 * lon_count) ** (-0.5)), shape(2, HQ, WT, kind=F32)

time: 122 us -> 121 us (level)
  waiting for transfers between devices: 41 us -> 39.7 us
  transfers between devices with their start and end apart: 12 -> 12, of which waited for: 5 -> 5; matrix products, arithmetic and copies ran while one was open for 1% -> 1% of each run, Pallas kernels for 16% -> 17%
where the time goes in v3:
time: 121 us
  Pallas kernels  42.4 us (35%)
  waiting for transfers between devices  39.7 us (33%)
  starting transfers between devices  34.3 us (28%)
  local copies, waits for them, and re-layouts  3.12 us (3%)
    ppermute x8, waiting for transfers between devices, move(): return lax.ppermute(block, ('lon',) + LAT, route)  23 us
    ppermute x8, starting transfers between devices, move(): return lax.ppermute(block, ('lon',) + LAT, route)  20.5 us
    all_to_all x2, waiting for transfers between devices, body(): grads = lax.all_to_all(grads, peers, 0, 0)  16.6 us
    pallas_call x1, Pallas kernels, body(): first_call()  16.3 us
    all_to_all x2, starting transfers between devices, body(): grads = lax.all_to_all(grads, peers, 0, 0)  12.8 us
    pallas_call x1, Pallas kernels, body(): grads, dqkv = second_call()(w3, wt3, w_proj, xn, datt, head, prob)  8.42 us
    pallas_call x1, Pallas kernels, body(): third_call()(tok8, datt, dqkv, merged, g1, w_qkv, out_map(), merged_map())  5.13 us
    pallas_call x1, Pallas kernels, body(): call(prepare_kernel, (shape(3, D, D), shape(3, D, D), shape(2, WT, HQ, ki...  3.67 us
  transfers between devices with their start and end apart: 12, of which 5 were waited for; matrix products, arithmetic and copies ran while one was open for 1% of the time, Pallas kernels for 17%

profile of v3, /device:TPU:1, one launch (start us, length us, event | category | flops | bytes accessed | tf_op | source)
XLA Modules:
  0.0 120.6 jit_solution(10862013234196489600)
XLA Ops:
  0.6 2.7 %shard_map.323 = (bf16[4,240,192]{2,1,0:T(8,128)(2,1)}, bf16[272,192]{1,0:T(8,128)(2,1)}, bf16[80,192]{1,0:T(8,128)(2,1)}, bf16[272,192]{1,0:T(8,128)(2,1)}, bf1...) custom-call(bf16[4,288,192]{2,1,0:T(8,128)(2,1)} %bitcast.21, bf16[72,4,384]{2,1,0:T(4,128)(2,1)} %bitcast.23, ...), custom_call_target="tpu_custom_call" | custom-call | flops 10000000 | bytes 1000000 | tf_op jit(solution)/shard_map/pallas_call | solution.py:789
  3.4 1.4 %collective-permute-start = (bf16[4,240,192]{2,1,0:T(8,128)(2,1)}, bf16[4,240,192]{2,1,0:T(8,128)(2,1)S(1)}, u32[]{:S(2)}, u32[]{:S(2)}) collective-permute-start(bf16[4,240,192]{2,1,0:T(8,128)(2,1)} %get-tuple-element.47), channel_id=1, source_target_pairs={{0,15},{1,0},{2,1},{3,2},{4,3},{5,4},{6,5},{7,6},{8,7},{9,8},{10,9... | collective-permute-start | bytes 1105928 | tf_op jit(solution)/shard_map/ppermute | solution.py:787
  4.8 5.9 %collective-permute-start.1 = (bf16[272,192]{1,0:T(8,128)(2,1)}, bf16[272,192]{1,0:T(8,128)(2,1)S(1)}, u32[]{:S(2)}, u32[]{:S(2)}) collective-permute-start(bf16[272,192]{1,0:T(8,128)(2,1)} %get-tuple-element.48), channel_id=1, source_target_pairs={{0,112},{1,113},{2,114},{3,115},{4,116},{5,117},{6,118},{7,119},{8... | collective-permute-start | bytes 313352 | tf_op jit(solution)/shard_map/ppermute | solution.py:787
  10.7 3.4 %collective-permute-start.3 = (bf16[272,192]{1,0:T(8,128)(2,1)}, bf16[272,192]{1,0:T(8,128)(2,1)S(1)}, u32[]{:S(2)}, u32[]{:S(2)}) collective-permute-start(bf16[272,192]{1,0:T(8,128)(2,1)} %get-tuple-element.50), channel_id=1, source_target_pairs={{0,127},{1,112},{2,113},{3,114},{4,115},{5,116},{6,117},{7,118},{8... | collective-permute-start | bytes 313352 | tf_op jit(solution)/shard_map/ppermute | solution.py:787
  14.1 3.2 %collective-permute-start.2 = (bf16[80,192]{1,0:T(8,128)(2,1)}, bf16[80,192]{1,0:T(8,128)(2,1)S(1)}, u32[]{:S(2)}, u32[]{:S(2)}) collective-permute-start(bf16[80,192]{1,0:T(8,128)(2,1)} %get-tuple-element.49), channel_id=1, source_target_pairs={{0,16},{1,17},{2,18},{3,19},{4,20},{5,21},{6,22},{7,23},{8,24},{9,... | collective-permute-start | bytes 92168 | tf_op jit(solution)/shard_map/ppermute | solution.py:787
  17.3 0.0 collective-permute-start.4
  17.3 1.3 %reshape.67.refs_26_ = f32[1,768]{1,0:T(1,128)} reshape(f32[768]{0:T(1024)} %param.36) | data formatting | bytes 6144 | tf_op jit(solution)/shard_map/reshape | solution.py:821
  18.6 3.7 %shard_map.324 = (bf16[3,192,192]{2,1,0:T(8,128)(2,1)}, bf16[3,192,192]{2,1,0:T(8,128)(2,1)}, f32[2,144,864]{2,1,0:T(8,128)}, f32[2,2,144,144]{3,2,1,0:T(8,128)}) custom-call(s32[1,1]{1,0:T(1,128)} %bitcast.5.bottom_ref, bf16[192,576]{1,0:T(8,128)(2,1)} %wqkv.3, f32[2,864,144]{2,1,0:T(8,128)} %bitcast.20), custom_call_target="tpu_custom_call" | custom-call | flops 10000000 | bytes 1000000 | tf_op jit(solution)/shard_map/pallas_call | solution.py:810
  22.3 0.0 collective-permute-done.2.refs_4_
  22.3 0.0 copy-start.9
  22.3 2.0 %collective-permute-done.4.refs_6_ = bf16[80,192]{1,0:T(8,128)(2,1)S(1)} collective-permute-done((bf16[80,192]{1,0:T(8,128)(2,1)}, bf16[80,192]{1,0:T(8,128)(2,1)S(1)}, u32[]{:S(2)}, u32[]{:S(2)}) %collective-permute-start.4) | collective-permute-done | bytes 30752 | tf_op jit(solution)/shard_map/ppermute | solution.py:787
  24.3 0.0 copy-start.10
  24.3 0.0 collective-permute-done.1.refs_3_
  24.3 0.0 copy-start.7
  24.3 0.0 collective-permute-done.3.refs_5_
  24.3 0.0 copy-start.8
  24.3 0.0 collective-permute-done.refs_2_
  24.3 0.0 copy-start.5
  24.3 0.0 copy-done.9
  24.3 0.6 copy-done.10
  24.9 0.1 copy-done.7
  24.9 0.0 copy-done.8
  25.0 0.2 copy-done.5
  25.2 16.3 %shard_map.325 = (bf16[2560,128]{1,0:T(8,128)(2,1)}, bf16[2560,128]{1,0:T(8,128)(2,1)}, bf16[320,384]{1,0:T(8,128)(2,1)}, bf16[8,144,192]{2,1,0:T(8,128)(2,1)}, ...) custom-call(s32[1,1]{1,0:T(1,128)} %bitcast.refs_0_.core_ref, ...), custom_call_target="tpu_custom_call" | custom-call | flops 20000000000 | bytes 10000000 | tf_op jit(solution)/shard_map/pallas_call | solution.py:817
  41.5 0.1 collective-permute-start.5
  41.5 0.0 copy-start.4
  41.6 8.4 %shard_map.326 = (bf16[64,88,128]{2,1,0:T(8,128)(2,1)}, bf16[3,8,144,192]{3,2,1,0:T(8,128)(2,1)}) custom-call(bf16[3,192,192]{2,1,0:T(8,128)(2,1)} %get-tuple-element.52.refs_9_.refs_0_, bf16[3,192,192]{2,1,0:T(8,128)(2,1)} %get-tuple-element.53.refs_10_.refs_1_, bf16[192,192]{1,0:T(8,128)(2,1)} %refs_2_.1, bf16[8,144,192]{2,1,0:T(8,128)(2,1)} %get-tuple-element.58.refs_3_, ...), custom_call_target="tpu_custom_call" | custom-call | flops 10000000000 | bytes 10000000 | tf_op jit(solution)/shard_map/pallas_call | solution.py:824
  50.0 0.0 collective-permute-done.5
  50.0 0.0 copy-done.4
  50.0 0.2 add_convert_fusion
  50.2 1.0 constant_dynamic-update-slice_fusion
  51.2 7.4 %all-to-all-start = ((bf16[64,88,128]{2,1,0:T(8,128)(2,1)}), bf16[64,88,128]{2,1,0:T(8,128)(2,1)S(1)}, u32[]{:S(2)}, u32[]{:S(2)}) async-start(bf16[64,88,128]{2,1,0:T(8,128)(2,1)} %constant_dynamic-update-slice_fusion), calls=%async_computation | async-start | bytes 2883584 | tf_op jit(solution)/shard_map/all_to_all | solution.py:828
  58.6 5.1 %shard_map.327 = (bf16[4,144,192]{2,1,0:T(8,128)(2,1)}, bf16[4,48,384]{2,1,0:T(8,128)(2,1)}, bf16[4,64,192]{2,1,0:T(8,128)(2,1)}, bf16[4,240,192]{2,1,0:T(8,128)(2,1)}, bf16[4,64,192]{2,1,0:T(8,128)(2,1)}) custom-call(bf16[8,144,192]{2,1,0:T(8,128)(2,1)} %get-tuple-element.65.tok8, bf16[8,144,192]{2,1,0:T(8,128)(2,1)} %get-tuple-element.59.refs_4_.datt, ...), custom_call_target="tpu_custom_call" | custom-call | flops 10000000000 | bytes 10000000 | tf_op jit(solution)/shard_map/pallas_call | solution.py:829
  63.7 16.6 %all-to-all-done.got = bf16[64,88,128]{2,1,0:T(8,128)(2,1)S(1)} async-done(((bf16[64,88,128]{2,1,0:T(8,128)(2,1)}), bf16[64,88,128]{2,1,0:T(8,128)(2,1)S(1)}, u32[]{:S(2)}, u32[]{:S(2)}) %all-to-all-start) | async-done | bytes 1441824 | tf_op jit(solution)/shard_map/all_to_all | solution.py:828
  80.3 1.4 %shard_map.328 = bf16[64,88,128]{2,1,0:T(8,128)(2,1)} custom-call(s32[1,1]{1,0:T(1,128)} %bitcast.10.is_weight, bf16[64,88,128]{2,1,0:T(8,128)(2,1)S(1)} %all-to-all-done.got), custom_call_target="tpu_custom_call" | custom-call | flops 10000000 | bytes 1000000 | tf_op jit(solution)/shard_map/pallas_call | solution.py:836
  81.7 0.0 copy-start.6
  81.7 5.4 %all-to-all-start.1 = ((bf16[64,88,128]{2,1,0:T(8,128)(2,1)}), bf16[64,88,128]{2,1,0:T(8,128)(2,1)S(1)}, u32[]{:S(2)}, u32[]{:S(2)}) async-start(bf16[64,88,128]{2,1,0:T(8,128)(2,1)} %shard_map.328), calls=%async_computation.1 | async-start | bytes 2883584 | tf_op jit(solution)/shard_map/all_to_all | solution.py:839
  87.1 0.0 copy-done.6
  87.1 2.8 %collective-permute-start.7 = (bf16[4,240,192]{2,1,0:T(8,128)(2,1)S(1)}, bf16[4,240,192]{2,1,0:T(8,128)(2,1)S(1)}, u32[]{:S(2)}, u32[]{:S(2)}) collective-permute-start(bf16[4,240,192]{2,1,0:T(8,128)(2,1)S(1)} %copy-done.6), channel_id=1, source_target_pairs={{0,1},{1,2},{2,3},{3,4},{4,5},{5,6},{6,7},{7,8},{8,9},{9,10},{10,1... | collective-permute-start | bytes 1105928 | tf_op jit(solution)/shard_map/ppermute | solution.py:787
  89.9 2.4 %collective-permute-start.6 = (bf16[4,64,192]{2,1,0:T(8,128)(2,1)}, bf16[4,64,192]{2,1,0:T(8,128)(2,1)S(1)}, u32[]{:S(2)}, u32[]{:S(2)}) collective-permute-start(bf16[4,64,192]{2,1,0:T(8,128)(2,1)} %get-tuple-element.72), channel_id=1, source_target_pairs={{0,16},{1,17},{2,18},{3,19},{4,20},{5,21},{6,22},{7,23},{8,24},{9,... | collective-permute-start | bytes 294920 | tf_op jit(solution)/shard_map/ppermute | solution.py:787
  92.3 0.0 copy-start
  92.3 0.0 copy-start.1
  92.3 0.0 copy-start.2
  92.3 0.0 copy-start.3
  92.3 1.4 %collective-permute-start.8 = (bf16[4,64,192]{2,1,0:T(8,128)(2,1)}, bf16[4,64,192]{2,1,0:T(8,128)(2,1)S(1)}, u32[]{:S(2)}, u32[]{:S(2)}) collective-permute-start(bf16[4,64,192]{2,1,0:T(8,128)(2,1)} %get-tuple-element.74), channel_id=1, source_target_pairs={{0,17},{1,18},{2,19},{3,20},{4,21},{5,22},{6,23},{7,24},{8,25},{9,... | collective-permute-start | bytes 294920 | tf_op jit(solution)/shard_map/ppermute | solution.py:787
  93.7 20.4 %collective-permute-done.6.rt = bf16[4,64,192]{2,1,0:T(8,128)(2,1)S(1)} collective-permute-done((bf16[4,64,192]{2,1,0:T(8,128)(2,1)}, bf16[4,64,192]{2,1,0:T(8,128)(2,1)S(1)}, u32[]{:S(2)}, u32[]{:S(2)}) %collective-permute-start.6) | collective-permute-done | bytes 98336 | tf_op jit(solution)/shard_map/ppermute | solution.py:787
  114.1 0.6 collective-permute-done.8.dr
  114.7 0.0 collective-permute-done.7.dn
  114.7 0.0 all-to-all-done.1.buf
  114.7 0.9 collective-permute-start.9
  115.7 1.5 %shard_map.331 = f32[2,864,144]{2,1,0:T(8,128)} custom-call(bf16[64,88,128]{2,1,0:T(8,128)(2,1)S(1)} %all-to-all-done.1.buf), custom_call_target="tpu_custom_call" | custom-call | flops 10000000 | bytes 1000000 | tf_op jit(solution)/shard_map/pallas_call | solution.py:845
  117.2 0.0 copy-done
  117.2 0.0 copy-done.1
  117.2 0.0 copy-done.2
  117.2 0.0 copy-done.3
  117.2 1.2 shard_map.329
  118.4 0.1 collective-permute-done.9.oth
  118.5 2.1 %shard_map.330 = (f32[192,576]{1,0:T(8,128)}, f32[192,192]{1,0:T(8,128)}, f32[192,768]{1,0:T(8,128)}, f32[192,768]{1,0:T(8,128)}, f32[768,384]{1,0:T(8,128)}) custom-call(s32[1,1]{1,0:T(1,128)} %bitcast.refs_0_.core_ref, bf16[64,88,128]{2,1,0:T(8,128)(2,1)S(1)} %all-to-all-done.1.buf, bf16[64,88,128]{2,1,0:T(8,128)(2,1)S(1)} %collective-permute-done.9.oth), custom_call_target="tpu_custom_call" | custom-call | flops 10000000 | bytes 1000000 | tf_op jit(solution)/shard_map/pallas_call | solution.py:848
Async XLA Ops:
  3.4 20.9 %collective-permute-start = (bf16[4,240,192]{2,1,0:T(8,128)(2,1)}, bf16[4,240,192]{2,1,0:T(8,128)(2,1)S(1)}, u32[]{:S(2)}, u32[]{:S(2)}) collective-permute-start(bf16[4,240,192]{2,1,0:T(8,128)(2,1)} %get-tuple-element.47), channel_id=1, source_target_pairs={{0,15},{1,0},{2,1},{3,2},{4,3},{5,4},{6,5},{7,6},{8,7},{9,8},{10,9... | collective-permute-start | bytes 1105928 | tf_op jit(solution)/shard_map/ppermute | solution.py:787
  4.8 19.5 %collective-permute-start.1 = (bf16[272,192]{1,0:T(8,128)(2,1)}, bf16[272,192]{1,0:T(8,128)(2,1)S(1)}, u32[]{:S(2)}, u32[]{:S(2)}) collective-permute-start(bf16[272,192]{1,0:T(8,128)(2,1)} %get-tuple-element.48), channel_id=1, source_target_pairs={{0,112},{1,113},{2,114},{3,115},{4,116},{5,117},{6,118},{7,119},{8... | collective-permute-start | bytes 313352 | tf_op jit(solution)/shard_map/ppermute | solution.py:787
  10.7 13.6 %collective-permute-start.3 = (bf16[272,192]{1,0:T(8,128)(2,1)}, bf16[272,192]{1,0:T(8,128)(2,1)S(1)}, u32[]{:S(2)}, u32[]{:S(2)}) collective-permute-start(bf16[272,192]{1,0:T(8,128)(2,1)} %get-tuple-element.50), channel_id=1, source_target_pairs={{0,127},{1,112},{2,113},{3,114},{4,115},{5,116},{6,117},{7,118},{8... | collective-permute-start | bytes 313352 | tf_op jit(solution)/shard_map/ppermute | solution.py:787
  14.1 8.2 %collective-permute-start.2 = (bf16[80,192]{1,0:T(8,128)(2,1)}, bf16[80,192]{1,0:T(8,128)(2,1)S(1)}, u32[]{:S(2)}, u32[]{:S(2)}) collective-permute-start(bf16[80,192]{1,0:T(8,128)(2,1)} %get-tuple-element.49), channel_id=1, source_target_pairs={{0,16},{1,17},{2,18},{3,19},{4,20},{5,21},{6,22},{7,23},{8,24},{9,... | collective-permute-start | bytes 92168 | tf_op jit(solution)/shard_map/ppermute | solution.py:787
  17.3 7.0 %collective-permute-start.4 = (bf16[80,192]{1,0:T(8,128)(2,1)}, bf16[80,192]{1,0:T(8,128)(2,1)S(1)}, u32[]{:S(2)}, u32[]{:S(2)}) collective-permute-start(bf16[80,192]{1,0:T(8,128)(2,1)} %get-tuple-element.51), channel_id=1, source_target_pairs={{0,31},{1,16},{2,17},{3,18},{4,19},{5,20},{6,21},{7,22},{8,23},{9,... | collective-permute-start | bytes 92168 | tf_op jit(solution)/shard_map/ppermute | solution.py:787
  22.3 2.1 %copy-start.9 = (bf16[80,192]{1,0:T(8,128)(2,1)}, bf16[80,192]{1,0:T(8,128)(2,1)S(1)}, u32[]{:S(2)}) copy-start(bf16[80,192]{1,0:T(8,128)(2,1)S(1)} %collective-permute-done.2.refs_4_) | copy-start | bytes 92164
  24.3 0.6 copy-start.10
  24.3 0.7 copy-start.7
  24.3 0.7 copy-start.8
  24.3 0.8 copy-start.5
  41.5 8.5 %collective-permute-start.5 = (bf16[2560,128]{1,0:T(8,128)(2,1)}, bf16[2560,128]{1,0:T(8,128)(2,1)S(1)}, u32[]{:S(2)}, u32[]{:S(2)}) collective-permute-start(bf16[2560,128]{1,0:T(8,128)(2,1)} %get-tuple-element.57), channel_id=1, source_target_pairs={{0,1},{1,0},{2,3},{3,2},{4,5},{5,4},{6,7},{7,6},{8,9},{9,8},{10,11... | collective-permute-start | bytes 1966088 | tf_op jit(solution)/shard_map/ppermute | solution.py:823
  41.5 8.5 %copy-start.4 = (bf16[2560,128]{1,0:T(8,128)(2,1)S(1)}, bf16[2560,128]{1,0:T(8,128)(2,1)}, u32[]{:S(2)}) copy-start(bf16[2560,128]{1,0:T(8,128)(2,1)} %get-tuple-element.63) | copy-start | bytes 1966084
  51.2 29.1 %all-to-all-start = ((bf16[64,88,128]{2,1,0:T(8,128)(2,1)}), bf16[64,88,128]{2,1,0:T(8,128)(2,1)S(1)}, u32[]{:S(2)}, u32[]{:S(2)}) async-start(bf16[64,88,128]{2,1,0:T(8,128)(2,1)} %constant_dynamic-update-slice_fusion), calls=%async_computation | async-start | bytes 2883584 | tf_op jit(solution)/shard_map/all_to_all | solution.py:828
  81.7 5.4 %copy-start.6 = (bf16[4,240,192]{2,1,0:T(8,128)(2,1)S(1)}, bf16[4,240,192]{2,1,0:T(8,128)(2,1)}, u32[]{:S(2)}) copy-start(bf16[4,240,192]{2,1,0:T(8,128)(2,1)} %get-tuple-element.73) | copy-start | bytes 1105924
  81.7 33.0 %all-to-all-start.1 = ((bf16[64,88,128]{2,1,0:T(8,128)(2,1)}), bf16[64,88,128]{2,1,0:T(8,128)(2,1)S(1)}, u32[]{:S(2)}, u32[]{:S(2)}) async-start(bf16[64,88,128]{2,1,0:T(8,128)(2,1)} %shard_map.328), calls=%async_computation.1 | async-start | bytes 2883584 | tf_op jit(solution)/shard_map/all_to_all | solution.py:839
  87.1 27.6 %collective-permute-start.7 = (bf16[4,240,192]{2,1,0:T(8,128)(2,1)S(1)}, bf16[4,240,192]{2,1,0:T(8,128)(2,1)S(1)}, u32[]{:S(2)}, u32[]{:S(2)}) collective-permute-start(bf16[4,240,192]{2,1,0:T(8,128)(2,1)S(1)} %copy-done.6), channel_id=1, source_target_pairs={{0,1},{1,2},{2,3},{3,4},{4,5},{5,6},{6,7},{7,8},{8,9},{9,10},{10,1... | collective-permute-start | bytes 1105928 | tf_op jit(solution)/shard_map/ppermute | solution.py:787
  89.9 24.3 %collective-permute-start.6 = (bf16[4,64,192]{2,1,0:T(8,128)(2,1)}, bf16[4,64,192]{2,1,0:T(8,128)(2,1)S(1)}, u32[]{:S(2)}, u32[]{:S(2)}) collective-permute-start(bf16[4,64,192]{2,1,0:T(8,128)(2,1)} %get-tuple-element.72), channel_id=1, source_target_pairs={{0,16},{1,17},{2,18},{3,19},{4,20},{5,21},{6,22},{7,23},{8,24},{9,... | collective-permute-start | bytes 294920 | tf_op jit(solution)/shard_map/ppermute | solution.py:787
  92.3 24.9 %copy-start = (bf16[288,512]{1,0:T(8,128)(2,1)S(1)}, bf16[288,512]{1,0:T(8,128)(2,1)}, u32[]{:S(2)}) copy-start(bf16[288,512]{1,0:T(8,128)(2,1)} %constant.74.clone.m_pm) | copy-start | bytes 884740
  92.3 24.9 %copy-start.1 = (bf16[4,144,192]{2,1,0:T(8,128)(2,1)S(1)}, bf16[4,144,192]{2,1,0:T(8,128)(2,1)}, u32[]{:S(2)}) copy-start(bf16[4,144,192]{2,1,0:T(8,128)(2,1)} %get-tuple-element.69.keep_t) | copy-start | bytes 663556
  92.3 24.9 %copy-start.2 = (bf16[4,48,384]{2,1,0:T(8,128)(2,1)S(1)}, bf16[4,48,384]{2,1,0:T(8,128)(2,1)}, u32[]{:S(2)}) copy-start(bf16[4,48,384]{2,1,0:T(8,128)(2,1)} %get-tuple-element.70.keep_m) | copy-start | bytes 442372
  92.3 24.9 %copy-start.3 = (bf16[144,32]{1,0:T(8,128)(2,1)S(1)}, bf16[144,32]{1,0:T(8,128)(2,1)}, u32[]{:S(2)}) copy-start(bf16[144,32]{1,0:T(8,128)(2,1)} %constant.73.clone.m_place) | copy-start | bytes 27652
  92.3 22.4 %collective-permute-start.8 = (bf16[4,64,192]{2,1,0:T(8,128)(2,1)}, bf16[4,64,192]{2,1,0:T(8,128)(2,1)S(1)}, u32[]{:S(2)}, u32[]{:S(2)}) collective-permute-start(bf16[4,64,192]{2,1,0:T(8,128)(2,1)} %get-tuple-element.74), channel_id=1, source_target_pairs={{0,17},{1,18},{2,19},{3,20},{4,21},{5,22},{6,23},{7,24},{8,25},{9,... | collective-permute-start | bytes 294920 | tf_op jit(solution)/shard_map/ppermute | solution.py:787
  114.7 3.8 %collective-permute-start.9 = (bf16[64,88,128]{2,1,0:T(8,128)(2,1)S(1)}, bf16[64,88,128]{2,1,0:T(8,128)(2,1)S(1)}, u32[]{:S(2)}, u32[]{:S(2)}) collective-permute-start(bf16[64,88,128]{2,1,0:T(8,128)(2,1)S(1)} %all-to-all-done.1.buf), channel_id=1, source_target_pairs={{0,1},{1,0},{2,3},{3,2},{4,5},{5,4},{6,7},{7,6},{8,9},{9,8},{10,11... | collective-permute-start | bytes 4325384 | tf_op jit(solution)/shard_map/ppermute | solution.py:844
